TPU v7x, 256 devices: a whole 4x4x8 slice. The times are simulated.
256 devices in a mesh: gx: 32 (over y, z_lo, core), gy: 8 (over z_hi, x).
Axes of the slice: x: 4, y: 4, z: 8 (z_hi: 2, z_lo: 4; z = z_hi * 4 + z_lo), core: 2. Of those that a mesh axis runs over, the one named last changes fastest.
Arguments:
- c_start: float32 [12, 32, 16, 1024], P(None, 'gx', None, 'gy'), may hold values from -6 to 6
- log_tort: float32 [32, 16, 1024], P('gx', None, 'gy'), may hold values from -0.7 to 0.7
- direction: float32 [32, 16, 1024], P('gx', None, 'gy'), may hold values from -3 to 5
- mix_inverse: float32 [4, 12, 12], replicated, may hold values from -0.055 to 1
- pair_mask: int32 [12, 12], replicated, may hold values 0 or 1
- soil_layer: int32 [32, 1024], P('gx', 'gy'), may hold values from 0 to 3
- observed: float32 [12, 32, 1024], P(None, 'gx', 'gy'), may hold values from -9 to 9
Outputs:
- hess_vec: float32 [32, 16, 1024], P('gx', None, 'gy')
All inputs are finite; a program needn't handle non-finite values.
Results may differ from a plain program's by a relative error of at most 0.00014.
Values sent between devices are 32-bit elements; how exact they have to be, the bound alone decides.
A program may use at most 64 MiB of HBM per device.

v0:
```python
import jax
import jax.numpy as jnp
from jax import lax
from jax.sharding import PartitionSpec as P

STEPS = 3


DT = 0.04
NEIGHBOURS = ((1, 0, 0), (-1, 0, 0), (0, 1, 0), (0, -1, 0), (0, 0, 1), (0, 0, -1))


def passed_along(block, axis, distance):
    devices = range(lax.axis_size(axis))
    route = [(i - distance, i) for i in devices if i - distance in devices]
    return lax.ppermute(block, axis, route)


def with_halo(value, sides, width):
    for axis, dim in sides:
        devices, length = (lax.axis_size(axis), value.shape[dim])
        up = [(i, (i + 1) % devices) for i in range(devices - 1)]
        down = [(j, i) for i, j in up]
        last = lax.slice_in_dim(value, length - width, length, axis=dim)
        first = lax.slice_in_dim(value, 0, width, axis=dim)
        before = lax.ppermute(last, axis, up)
        after = lax.ppermute(first, axis, down)
        value = jnp.concatenate([before, value, after], axis=dim)
    return value


def window(array, shift_x, shift_z, shift_y):
    extent = array.shape[-3:]
    return array[
        ...,
        1 + shift_x : extent[0] - 1 + shift_x,
        1 + shift_z : extent[1] - 1 + shift_z,
        1 + shift_y : extent[2] - 1 + shift_y,
    ]


def advance(state_pad, tort_pad, mixers, masks):
    coeff = jnp.exp(tort_pad)
    center = window(state_pad, 0, 0, 0)
    middle = window(coeff, 0, 0, 0)
    spread = jnp.zeros_like(center)
    for shift_x, shift_z, shift_y in NEIGHBOURS:
        face = 0.5 * (middle + window(coeff, shift_x, shift_z, shift_y))
        spread = spread + face * (window(state_pad, shift_x, shift_z, shift_y) - center)
    mixed = jnp.zeros_like(center)
    for level in range(mixers.shape[0]):
        mixed = mixed + masks[level] * jnp.einsum(
            "st,txzy->sxzy", mixers[level], spread, precision=lax.Precision.HIGHEST
        )
    return center + DT * mixed


def effective_mixers(mix_inverse, pair_mask):
    count = mix_inverse.shape[1]
    diagonal = lax.broadcasted_iota(jnp.int32, (count, count), 0) == lax.broadcasted_iota(
        jnp.int32, (count, count), 1
    )
    return jnp.where(diagonal[None], mix_inverse, mix_inverse * pair_mask.astype(jnp.float32)[None])


def layer_masks(soil_layer, levels):
    return (
        soil_layer[None, :, None, :] == jnp.arange(levels, dtype=jnp.int32)[:, None, None, None]
    ).astype(jnp.float32)


def pad_depth(array):
    widths = [(0, 0)] * (array.ndim - 2) + [(1, 1), (0, 0)]
    return jnp.pad(array, widths)


def fold_ghosts(stacked):
    inner = stacked[:, 1:-1, :, 1:-1]
    from_above = passed_along(stacked[:, 0, :, 1:-1], "gx", -1)
    from_below = passed_along(stacked[:, -1, :, 1:-1], "gx", 1)
    inner = inner.at[:, -1].add(from_above)
    inner = inner.at[:, 0].add(from_below)
    from_right = passed_along(stacked[:, 1:-1, :, 0], "gy", -1)
    from_left = passed_along(stacked[:, 1:-1, :, -1], "gy", 1)
    inner = inner.at[:, :, :, -1].add(from_right)
    inner = inner.at[:, :, :, 0].add(from_left)
    return inner


def body(c_start, log_tort, direction, mix_inverse, pair_mask, soil_layer, observed):
    mixers = effective_mixers(mix_inverse, pair_mask)
    masks = layer_masks(soil_layer, mix_inverse.shape[0])
    species = c_start.shape[0]
    count = (
        species * c_start.shape[1] * c_start.shape[3] * lax.axis_size("gx") * lax.axis_size("gy")
    )

    def forward(state_pad, tort_pad):
        return advance(state_pad, tort_pad, mixers, masks)

    both_fields = with_halo(jnp.stack([log_tort, direction]), (("gx", 1), ("gy", 3)), 1)
    both_fields = pad_depth(both_fields)
    tort_pad = both_fields[0]
    dir_pad = both_fields[1]
    state = c_start
    tangent = jnp.zeros_like(c_start)
    state_pads = []
    tangent_pads = []
    for moment in range(STEPS):
        state_pad = pad_depth(with_halo(state, (("gx", 1), ("gy", 3)), 1))
        state_pads.append(state_pad)
        state = forward(state_pad, tort_pad)
    mismatch = state[:, :, 0, :] - observed
    total = lax.psum(jnp.sum(mismatch * mismatch), ("gx", "gy"))
    for moment in range(STEPS):
        tangent_pad = pad_depth(with_halo(tangent, (("gx", 1), ("gy", 3)), 1))
        tangent_pads.append(tangent_pad)
        tangent = jax.jvp(forward, (state_pads[moment], tort_pad), (tangent_pad, dir_pad))[1]
    mismatch_dot = tangent[:, :, 0, :]
    cross = lax.psum(jnp.sum(mismatch * mismatch_dot), ("gx", "gy"))
    factor = count / total
    top_adjoint = factor * mismatch
    top_second = factor * mismatch_dot - 2.0 * count * cross / (total * total) * mismatch
    below = jnp.zeros(
        (species, c_start.shape[1], c_start.shape[2] - 1, c_start.shape[3]), jnp.float32
    )
    adjoint = jnp.concatenate([top_adjoint[:, :, None, :], below], 2)
    second_adjoint = jnp.concatenate([top_second[:, :, None, :], below], 2)
    hess_vec = jnp.zeros_like(log_tort)

    def pullback(state_pad, tort_field, weights):
        outcome, back = jax.vjp(forward, state_pad, tort_field)
        return back(weights)

    for moment in reversed(range(STEPS)):
        grads, tangents = jax.jvp(
            pullback,
            (state_pads[moment], tort_pad, adjoint),
            (tangent_pads[moment], dir_pad, second_adjoint),
        )
        stacked = jnp.concatenate([grads[0], tangents[0], tangents[1][None]], 0)[:, :, 1:-1, :]
        folded = fold_ghosts(stacked)
        adjoint = folded[:species]
        second_adjoint = folded[species : 2 * species]
        hess_vec = hess_vec + folded[2 * species]
    return hess_vec


def solution(mesh):
    return jax.shard_map(
        body,
        mesh=mesh,
        in_specs=(
            P(None, "gx", None, "gy"),
            P("gx", None, "gy"),
            P("gx", None, "gy"),
            P(),
            P(),
            P("gx", "gy"),
            P(None, "gx", "gy"),
        ),
        out_specs=P("gx", None, "gy"),
        check_vma=False,
    )
```

profile of v0, /device:TPU:14, one launch (start us, length us, event | category | flops | bytes accessed | tf_op | source)
XLA Modules:
  0.0 398.6 jit_solution(13227775361925297021)
XLA Ops:
  0.7 5.8 %collective-permute-start.1 = (f32[2,1,16,128]{3,2,1,0:T(8,128)S(1)}, f32[2,1,16,128]{3,2,1,0:T(8,128)S(1)}, u32[]{:S(2)}, u32[]{:S(2)}) collective-permute-start(f32[2,1,16,128]{3,2,1,0:T(8,128)S(1)} %pad_maximum_fusion.44), channel_id=1, source_target_pairs={{8,0},{16,8},{24,16},{32,24},{40,32},{48,40},{56,48},{64,56},{72,6... | collective-permute-start | bytes 49160 | tf_op jit(solution)/shard_map/ppermute | solution.py:27
  6.6 1.9 collective-permute-start
  9.4 6.3 %collective-permute-start.4 = (f32[12,1,16,128]{3,0,2,1:T(8,128)S(1)}, f32[12,1,16,128]{3,0,2,1:T(8,128)S(1)}, u32[]{:S(2)}, u32[]{:S(2)}) collective-permute-start(f32[12,1,16,128]{3,0,2,1:T(8,128)S(1)} %copy.1234), channel_id=1, source_target_pairs={{8,0},{16,8},{24,16},{32,24},{40,32},{48,40},{56,48},{64,56},{72,6... | collective-permute-start | bytes 294920 | tf_op jit(solution)/shard_map/ppermute | solution.py:27
  15.8 1.9 collective-permute-start.5
  17.8 1.9 collective-permute-start.17
  21.2 6.3 %collective-permute-start.2 = (f32[2,3,16,1]{3,2,1,0:T(8,128)S(1)}, f32[2,3,16,1]{3,2,1,0:T(8,128)S(1)}, u32[]{:S(2)}, u32[]{:S(2)}) collective-permute-start(f32[2,3,16,1]{3,2,1,0:T(8,128)S(1)} %get-tuple-element.316), channel_id=1, source_target_pairs={{0,1},{1,2},{2,3},{3,4},{4,5},{5,6},{6,7},{8,9},{9,10},{10,11},{11... | collective-permute-start | bytes 1160 | tf_op jit(solution)/shard_map/ppermute | solution.py:26
  27.5 1.9 collective-permute-start.3
  29.4 6.1 %collective-permute-start.16 = (f32[12,1,16,128]{3,0,2,1:T(8,128)S(1)}, f32[12,1,16,128]{3,0,2,1:T(8,128)S(1)}, u32[]{:S(2)}, u32[]{:S(2)}) collective-permute-start(f32[12,1,16,128]{3,0,2,1:T(8,128)S(1)} %broadcast_in_dim.22), channel_id=1, source_target_pairs={{8,0},{16,8},{24,16},{32,24},{40,32},{48,40},{56,48},{64,56},{72,6... | collective-permute-start | bytes 294920 | tf_op jit(solution)/shard_map/ppermute | solution.py:27
  35.5 4.0 collective-permute-done.3
  41.1 7.7 %collective-permute-start.18 = (f32[12,3,16,1]{3,0,2,1:T(8,128)S(1)}, f32[12,3,16,1]{3,0,2,1:T(8,128)S(1)}, u32[]{:S(2)}, u32[]{:S(2)}) collective-permute-start(f32[12,3,16,1]{3,0,2,1:T(8,128)S(1)} %get-tuple-element.295), channel_id=1, source_target_pairs={{0,1},{1,2},{2,3},{3,4},{4,5},{5,6},{6,7},{8,9},{9,10},{10,11},{11... | collective-permute-start | bytes 6920 | tf_op jit(solution)/shard_map/ppermute | solution.py:26
  48.8 1.9 collective-permute-start.19
  51.0 9.9 %collective-permute-start.6 = (f32[12,3,16,1]{3,0,2,1:T(8,128)S(1)}, f32[12,3,16,1]{3,0,2,1:T(8,128)S(1)}, u32[]{:S(2)}, u32[]{:S(2)}) collective-permute-start(f32[12,3,16,1]{3,0,2,1:T(8,128)S(1)} %get-tuple-element.293), channel_id=1, source_target_pairs={{0,1},{1,2},{2,3},{3,4},{4,5},{5,6},{6,7},{8,9},{9,10},{10,11},{11... | collective-permute-start | bytes 6920 | tf_op jit(solution)/shard_map/ppermute | solution.py:26
  60.9 1.9 collective-permute-start.7
  62.8 1.8 collective-permute-done.19
  65.0 1.2 collective-permute-done.6
  66.2 10.5 %collective-permute-done.7 = f32[12,3,16,1]{3,0,2,1:T(8,128)S(1)} collective-permute-done((f32[12,3,16,1]{3,0,2,1:T(8,128)S(1)}, f32[12,3,16,1]{3,0,2,1:T(8,128)S(1)}, u32[]{:S(2)}, u32[]{:S(2)}) %collective-permute-start.7) | collective-permute-done | bytes 2336 | tf_op jit(solution)/shard_map/ppermute | solution.py:27
  80.2 1.9 collective-permute-start.21
  82.2 6.7 %collective-permute-start.20 = (f32[12,1,16,128]{3,0,2,1:T(8,128)S(1)}, f32[12,1,16,128]{3,0,2,1:T(8,128)S(1)}, u32[]{:S(2)}, u32[]{:S(2)}) collective-permute-start(f32[12,1,16,128]{3,0,2,1:T(8,128)S(1)} %bitcast.552), channel_id=1, source_target_pairs={{8,0},{16,8},{24,16},{32,24},{40,32},{48,40},{56,48},{64,56},{72,6... | collective-permute-start | bytes 294920 | tf_op jit(solution)/shard_map/ppermute | solution.py:27
  89.1 10.5 %collective-permute-start.9 = (f32[12,1,16,128]{3,0,2,1:T(8,128)S(1)}, f32[12,1,16,128]{3,0,2,1:T(8,128)S(1)}, u32[]{:S(2)}, u32[]{:S(2)}) collective-permute-start(f32[12,1,16,128]{3,0,2,1:T(8,128)S(1)} %fusion.37), channel_id=1, source_target_pairs={{0,8},{8,16},{16,24},{24,32},{32,40},{40,48},{48,56},{56,64},{64,7... | collective-permute-start | bytes 294920 | tf_op jit(solution)/shard_map/ppermute | solution.py:26
  99.6 1.9 collective-permute-start.8
  101.8 1.9 collective-permute-start.22
  103.7 3.9 collective-permute-start.23
  107.9 7.9 %collective-permute-start.10 = (f32[12,3,16,1]{3,0,2,1:T(8,128)S(1)}, f32[12,3,16,1]{3,0,2,1:T(8,128)S(1)}, u32[]{:S(2)}, u32[]{:S(2)}) collective-permute-start(f32[12,3,16,1]{3,0,2,1:T(8,128)S(1)} %get-tuple-element.289), channel_id=1, source_target_pairs={{0,1},{1,2},{2,3},{3,4},{4,5},{5,6},{6,7},{8,9},{9,10},{10,11},{11... | collective-permute-start | bytes 6920 | tf_op jit(solution)/shard_map/ppermute | solution.py:26
  115.8 1.9 collective-permute-start.11
  117.8 5.2 %collective-permute-done.23 = f32[12,3,16,1]{3,0,2,1:T(8,128)S(1)} collective-permute-done((f32[12,3,16,1]{3,0,2,1:T(8,128)S(1)}, f32[12,3,16,1]{3,0,2,1:T(8,128)S(1)}, u32[]{:S(2)}, u32[]{:S(2)}) %collective-permute-start.23) | collective-permute-done | bytes 2336 | tf_op jit(solution)/shard_map/ppermute | solution.py:27
  123.4 9.7 %collective-permute-done.11 = f32[12,3,16,1]{3,0,2,1:T(8,128)S(1)} collective-permute-done((f32[12,3,16,1]{3,0,2,1:T(8,128)S(1)}, f32[12,3,16,1]{3,0,2,1:T(8,128)S(1)}, u32[]{:S(2)}, u32[]{:S(2)}) %collective-permute-start.11) | collective-permute-done | bytes 2336 | tf_op jit(solution)/shard_map/ppermute | solution.py:27
  133.5 1.2 add_add_fusion.1
  137.4 4.4 %collective-permute-start.25 = (f32[12,1,16,128]{3,0,2,1:T(8,128)S(1)}, f32[12,1,16,128]{3,0,2,1:T(8,128)S(1)}, u32[]{:S(2)}, u32[]{:S(2)}) collective-permute-start(f32[12,1,16,128]{3,0,2,1:T(8,128)S(1)} %bitcast.545), channel_id=1, source_target_pairs={{0,8},{8,16},{16,24},{24,32},{32,40},{40,48},{48,56},{56,64},{64,7... | collective-permute-start | bytes 294920 | tf_op jit(solution)/shard_map/ppermute | solution.py:26
  141.9 3.8 collective-permute-start.24
  146.0 15.2 %collective-permute-start.13 = (f32[12,1,16,128]{3,0,2,1:T(8,128)S(1)}, f32[12,1,16,128]{3,0,2,1:T(8,128)S(1)}, u32[]{:S(2)}, u32[]{:S(2)}) collective-permute-start(f32[12,1,16,128]{3,0,2,1:T(8,128)S(1)} %fusion.36), channel_id=1, source_target_pairs={{0,8},{8,16},{16,24},{24,32},{32,40},{40,48},{48,56},{56,64},{64,7... | collective-permute-start | bytes 294920 | tf_op jit(solution)/shard_map/ppermute | solution.py:26
  161.2 1.9 collective-permute-start.12
  163.4 1.9 collective-permute-start.26
  165.3 3.9 collective-permute-start.27
  169.5 7.9 %collective-permute-start.14 = (f32[12,3,16,1]{3,0,2,1:T(8,128)S(1)}, f32[12,3,16,1]{3,0,2,1:T(8,128)S(1)}, u32[]{:S(2)}, u32[]{:S(2)}) collective-permute-start(f32[12,3,16,1]{3,0,2,1:T(8,128)S(1)} %get-tuple-element.285), channel_id=1, source_target_pairs={{0,1},{1,2},{2,3},{3,4},{4,5},{5,6},{6,7},{8,9},{9,10},{10,11},{11... | collective-permute-start | bytes 6920 | tf_op jit(solution)/shard_map/ppermute | solution.py:26
  177.4 1.9 collective-permute-start.15
  179.4 5.2 %collective-permute-done.27 = f32[12,3,16,1]{3,0,2,1:T(8,128)S(1)} collective-permute-done((f32[12,3,16,1]{3,0,2,1:T(8,128)S(1)}, f32[12,3,16,1]{3,0,2,1:T(8,128)S(1)}, u32[]{:S(2)}, u32[]{:S(2)}) %collective-permute-start.27) | collective-permute-done | bytes 2336 | tf_op jit(solution)/shard_map/ppermute | solution.py:27
  186.0 10.8 %collective-permute-done.15 = f32[12,3,16,1]{3,0,2,1:T(8,128)S(1)} collective-permute-done((f32[12,3,16,1]{3,0,2,1:T(8,128)S(1)}, f32[12,3,16,1]{3,0,2,1:T(8,128)S(1)}, u32[]{:S(2)}, u32[]{:S(2)}) %collective-permute-start.15) | collective-permute-done | bytes 2336 | tf_op jit(solution)/shard_map/ppermute | solution.py:27
  201.8 84.7 %all-reduce.93 = (f32[]{:T(128)}, f32[]{:T(128)}) all-reduce(f32[]{:T(128)} %get-tuple-element.196, f32[]{:T(128)} %get-tuple-element.195), channel_id=1, replica_groups=mesh['gx'=32,'gy'=8] {'gx','gy'}, use_global_device_ids=true, to_apply=%region_1.2 | all-reduce | flops 2 | bytes 16 | tf_op jit(solution)/shard_map/psum | solution.py:114
  295.4 1.2 add_reduce_fusion.14
  299.7 5.4 %collective-permute-start.28 = (f32[25,16,128]{2,0,1:T(8,128)}, f32[25,16,128]{2,0,1:T(8,128)}, u32[]{:S(2)}, u32[]{:S(2)}) collective-permute-start(f32[25,16,128]{2,0,1:T(8,128)} %get-tuple-element.269), channel_id=1, source_target_pairs={{8,0},{16,8},{24,16},{32,24},{40,32},{48,40},{56,48},{64,56},{72,6... | collective-permute-start | bytes 614408 | tf_op jit(solution)/shard_map/ppermute | solution.py:16
  305.1 1.9 collective-permute-start.29
  307.4 5.2 %collective-permute-start.31 = (f32[25,1,16]{0,2,1:T(8,128)S(1)}, f32[25,1,16]{0,2,1:T(8,128)S(1)}, u32[]{:S(2)}, u32[]{:S(2)}) collective-permute-start(f32[25,1,16]{0,2,1:T(8,128)S(1)} %bitcast.564), channel_id=1, source_target_pairs={{0,1},{1,2},{2,3},{3,4},{4,5},{5,6},{6,7},{8,9},{9,10},{10,11},{11... | collective-permute-start | bytes 4808 | tf_op jit(solution)/shard_map/ppermute | solution.py:16
  312.7 1.9 collective-permute-start.30
  315.5 8.7 %collective-permute-done.30 = f32[25,1,16]{0,2,1:T(8,128)S(1)} collective-permute-done((f32[25,1,16]{0,2,1:T(8,128)S(1)}, f32[25,1,16]{0,2,1:T(8,128)S(1)}, u32[]{:S(2)}, u32[]{:S(2)}) %collective-permute-start.30) | collective-permute-done | bytes 1632 | tf_op jit(solution)/shard_map/ppermute | solution.py:16
  325.1 1.2 fusion.44
  326.5 1.4 scatter-add.20
  333.5 1.4 add_reduce_fusion.6
  337.3 4.9 %collective-permute-start.32 = (f32[25,16,128]{2,0,1:T(8,128)}, f32[25,16,128]{2,0,1:T(8,128)}, u32[]{:S(2)}, u32[]{:S(2)}) collective-permute-start(f32[25,16,128]{2,0,1:T(8,128)} %get-tuple-element.267), channel_id=1, source_target_pairs={{8,0},{16,8},{24,16},{32,24},{40,32},{48,40},{56,48},{64,56},{72,6... | collective-permute-start | bytes 614408 | tf_op jit(solution)/shard_map/ppermute | solution.py:16
  342.2 1.9 collective-permute-start.33
  345.1 2.1 collective-permute-start.35
  347.2 3.7 collective-permute-start.34
  350.9 1.6 copy.1256
  352.5 6.5 %collective-permute-done.34 = f32[25,1,16]{0,2,1:T(8,128)} collective-permute-done((f32[25,1,16]{0,2,1:T(8,128)}, f32[25,1,16]{0,2,1:T(8,128)}, u32[]{:S(2)}, u32[]{:S(2)}) %collective-permute-start.34) | collective-permute-done | bytes 1632 | tf_op jit(solution)/shard_map/ppermute | solution.py:16
  359.1 1.6 copy.1255
  360.7 1.3 fusion.42
  362.1 1.4 scatter-add.24
  369.0 1.2 add_reduce_fusion.2
  373.4 5.0 %collective-permute-start.36 = (f32[25,16,128]{2,0,1:T(8,128)}, f32[25,16,128]{2,0,1:T(8,128)S(1)}, u32[]{:S(2)}, u32[]{:S(2)}) collective-permute-start(f32[25,16,128]{2,0,1:T(8,128)} %get-tuple-element.265), channel_id=1, source_target_pairs={{8,0},{16,8},{24,16},{32,24},{40,32},{48,40},{56,48},{64,56},{72,6... | collective-permute-start | bytes 614408 | tf_op jit(solution)/shard_map/ppermute | solution.py:16
  378.4 1.9 collective-permute-start.37
  380.7 2.5 collective-permute-start.39
  383.2 3.4 collective-permute-start.38
  386.8 8.0 %collective-permute-done.38 = f32[25,1,16]{0,2,1:T(8,128)S(1)} collective-permute-done((f32[25,1,16]{0,2,1:T(8,128)S(1)}, f32[25,1,16]{0,2,1:T(8,128)S(1)}, u32[]{:S(2)}, u32[]{:S(2)}) %collective-permute-start.38) | collective-permute-done | bytes 1632 | tf_op jit(solution)/shard_map/ppermute | solution.py:16
  395.0 1.1 fusion.40
  396.3 1.4 scatter-add.26
  (386 shorter events, 49.8 us)
Async XLA Ops:
  0.7 20.2 %collective-permute-start.1 = (f32[2,1,16,128]{3,2,1,0:T(8,128)S(1)}, f32[2,1,16,128]{3,2,1,0:T(8,128)S(1)}, u32[]{:S(2)}, u32[]{:S(2)}) collective-permute-start(f32[2,1,16,128]{3,2,1,0:T(8,128)S(1)} %pad_maximum_fusion.44), channel_id=1, source_target_pairs={{8,0},{16,8},{24,16},{32,24},{40,32},{48,40},{56,48},{64,56},{72,6... | collective-permute-start | bytes 49160 | tf_op jit(solution)/shard_map/ppermute | solution.py:27
  6.6 14.4 %collective-permute-start = (f32[2,1,16,128]{3,2,1,0:T(8,128)S(1)}, f32[2,1,16,128]{3,2,1,0:T(8,128)S(1)}, u32[]{:S(2)}, u32[]{:S(2)}) collective-permute-start(f32[2,1,16,128]{3,2,1,0:T(8,128)S(1)} %pad_maximum_fusion.44), channel_id=1, source_target_pairs={{0,8},{8,16},{16,24},{24,32},{32,40},{40,48},{48,56},{56,64},{64,7... | collective-permute-start | bytes 49160 | tf_op jit(solution)/shard_map/ppermute | solution.py:26
  9.4 41.3 %collective-permute-start.4 = (f32[12,1,16,128]{3,0,2,1:T(8,128)S(1)}, f32[12,1,16,128]{3,0,2,1:T(8,128)S(1)}, u32[]{:S(2)}, u32[]{:S(2)}) collective-permute-start(f32[12,1,16,128]{3,0,2,1:T(8,128)S(1)} %copy.1234), channel_id=1, source_target_pairs={{8,0},{16,8},{24,16},{32,24},{40,32},{48,40},{56,48},{64,56},{72,6... | collective-permute-start | bytes 294920 | tf_op jit(solution)/shard_map/ppermute | solution.py:27
  15.8 24.4 %collective-permute-start.5 = (f32[12,1,16,128]{3,0,2,1:T(8,128)S(1)}, f32[12,1,16,128]{3,0,2,1:T(8,128)S(1)}, u32[]{:S(2)}, u32[]{:S(2)}) collective-permute-start(f32[12,1,16,128]{3,0,2,1:T(8,128)S(1)} %copy.1234), channel_id=1, source_target_pairs={{0,8},{8,16},{16,24},{24,32},{32,40},{40,48},{48,56},{56,64},{64,7... | collective-permute-start | bytes 294920 | tf_op jit(solution)/shard_map/ppermute | solution.py:26
  17.7 2.6 copy-start.96
  17.7 2.6 copy-start.95
  17.8 22.2 %collective-permute-start.17 = (f32[12,1,16,128]{3,0,2,1:T(8,128)S(1)}, f32[12,1,16,128]{3,0,2,1:T(8,128)S(1)}, u32[]{:S(2)}, u32[]{:S(2)}) collective-permute-start(f32[12,1,16,128]{3,0,2,1:T(8,128)S(1)} %broadcast_in_dim.22), channel_id=1, source_target_pairs={{0,8},{8,16},{16,24},{24,32},{32,40},{40,48},{48,56},{56,64},{64,7... | collective-permute-start | bytes 294920 | tf_op jit(solution)/shard_map/ppermute | solution.py:26
  21.2 8.3 %collective-permute-start.2 = (f32[2,3,16,1]{3,2,1,0:T(8,128)S(1)}, f32[2,3,16,1]{3,2,1,0:T(8,128)S(1)}, u32[]{:S(2)}, u32[]{:S(2)}) collective-permute-start(f32[2,3,16,1]{3,2,1,0:T(8,128)S(1)} %get-tuple-element.316), channel_id=1, source_target_pairs={{0,1},{1,2},{2,3},{3,4},{4,5},{5,6},{6,7},{8,9},{9,10},{10,11},{11... | collective-permute-start | bytes 1160 | tf_op jit(solution)/shard_map/ppermute | solution.py:26
  27.5 12.0 %collective-permute-start.3 = (f32[2,3,16,1]{3,2,1,0:T(8,128)S(1)}, f32[2,3,16,1]{3,2,1,0:T(8,128)S(1)}, u32[]{:S(2)}, u32[]{:S(2)}) collective-permute-start(f32[2,3,16,1]{3,2,1,0:T(8,128)S(1)} %get-tuple-element.317), channel_id=1, source_target_pairs={{1,0},{2,1},{3,2},{4,3},{5,4},{6,5},{7,6},{9,8},{10,9},{11,10},{12... | collective-permute-start | bytes 1160 | tf_op jit(solution)/shard_map/ppermute | solution.py:27
  29.4 10.5 %collective-permute-start.16 = (f32[12,1,16,128]{3,0,2,1:T(8,128)S(1)}, f32[12,1,16,128]{3,0,2,1:T(8,128)S(1)}, u32[]{:S(2)}, u32[]{:S(2)}) collective-permute-start(f32[12,1,16,128]{3,0,2,1:T(8,128)S(1)} %broadcast_in_dim.22), channel_id=1, source_target_pairs={{8,0},{16,8},{24,16},{32,24},{40,32},{48,40},{56,48},{64,56},{72,6... | collective-permute-start | bytes 294920 | tf_op jit(solution)/shard_map/ppermute | solution.py:27
  39.8 257.0 %copy-start.49 = (f32[16,128]{1,0:T(8,128)}, f32[16,128]{1,0:T(8,128)S(1)}, u32[]{:S(2)}) copy-start(f32[16,128]{1,0:T(8,128)S(1)} %get-tuple-element.308) | copy-start | bytes 24580
  39.8 257.0 %copy-start.52 = (f32[16,128]{1,0:T(8,128)}, f32[16,128]{1,0:T(8,128)S(1)}, u32[]{:S(2)}) copy-start(f32[16,128]{1,0:T(8,128)S(1)} %get-tuple-element.309) | copy-start | bytes 24580
  39.9 157.4 %copy-start.57 = (f32[16,128]{1,0:T(8,128)}, f32[16,128]{1,0:T(8,128)S(1)}, u32[]{:S(2)}) copy-start(f32[16,128]{1,0:T(8,128)S(1)} %get-tuple-element.310) | copy-start | bytes 24580
  39.9 157.4 %copy-start.61 = (f32[16,128]{1,0:T(8,128)}, f32[16,128]{1,0:T(8,128)S(1)}, u32[]{:S(2)}) copy-start(f32[16,128]{1,0:T(8,128)S(1)} %get-tuple-element.311) | copy-start | bytes 24580
  39.9 157.4 %copy-start.65 = (f32[16,128]{1,0:T(8,128)}, f32[16,128]{1,0:T(8,128)S(1)}, u32[]{:S(2)}) copy-start(f32[16,128]{1,0:T(8,128)S(1)} %get-tuple-element.312) | copy-start | bytes 24580
  39.9 157.4 %copy-start.69 = (f32[16,128]{1,0:T(8,128)}, f32[16,128]{1,0:T(8,128)S(1)}, u32[]{:S(2)}) copy-start(f32[16,128]{1,0:T(8,128)S(1)} %get-tuple-element.313) | copy-start | bytes 24580
  39.9 157.4 %copy-start.73 = (f32[16,128]{1,0:T(8,128)}, f32[16,128]{1,0:T(8,128)S(1)}, u32[]{:S(2)}) copy-start(f32[16,128]{1,0:T(8,128)S(1)} %get-tuple-element.314) | copy-start | bytes 24580
  39.9 157.4 %copy-start.77 = (f32[16,128]{1,0:T(8,128)}, f32[16,128]{1,0:T(8,128)S(1)}, u32[]{:S(2)}) copy-start(f32[16,128]{1,0:T(8,128)S(1)} %get-tuple-element.315) | copy-start | bytes 24580
  40.0 37.1 %copy-start.3 = (f32[12,1,16,128]{3,0,2,1:T(8,128)}, f32[12,1,16,128]{3,0,2,1:T(8,128)S(1)}, u32[]{:S(2)}) copy-start(f32[12,1,16,128]{3,0,2,1:T(8,128)S(1)} %collective-permute-done.16) | copy-start | bytes 294916
  41.1 21.7 %collective-permute-start.18 = (f32[12,3,16,1]{3,0,2,1:T(8,128)S(1)}, f32[12,3,16,1]{3,0,2,1:T(8,128)S(1)}, u32[]{:S(2)}, u32[]{:S(2)}) collective-permute-start(f32[12,3,16,1]{3,0,2,1:T(8,128)S(1)} %get-tuple-element.295), channel_id=1, source_target_pairs={{0,1},{1,2},{2,3},{3,4},{4,5},{5,6},{6,7},{8,9},{9,10},{10,11},{11... | collective-permute-start | bytes 6920 | tf_op jit(solution)/shard_map/ppermute | solution.py:26
  48.8 15.8 %collective-permute-start.19 = (f32[12,3,16,1]{3,0,2,1:T(8,128)S(1)}, f32[12,3,16,1]{3,0,2,1:T(8,128)S(1)}, u32[]{:S(2)}, u32[]{:S(2)}) collective-permute-start(f32[12,3,16,1]{3,0,2,1:T(8,128)S(1)} %get-tuple-element.296), channel_id=1, source_target_pairs={{1,0},{2,1},{3,2},{4,3},{5,4},{6,5},{7,6},{9,8},{10,9},{11,10},{12... | collective-permute-start | bytes 6920 | tf_op jit(solution)/shard_map/ppermute | solution.py:27
  51.0 15.2 %collective-permute-start.6 = (f32[12,3,16,1]{3,0,2,1:T(8,128)S(1)}, f32[12,3,16,1]{3,0,2,1:T(8,128)S(1)}, u32[]{:S(2)}, u32[]{:S(2)}) collective-permute-start(f32[12,3,16,1]{3,0,2,1:T(8,128)S(1)} %get-tuple-element.293), channel_id=1, source_target_pairs={{0,1},{1,2},{2,3},{3,4},{4,5},{5,6},{6,7},{8,9},{9,10},{10,11},{11... | collective-permute-start | bytes 6920 | tf_op jit(solution)/shard_map/ppermute | solution.py:26
  60.9 15.8 %collective-permute-start.7 = (f32[12,3,16,1]{3,0,2,1:T(8,128)S(1)}, f32[12,3,16,1]{3,0,2,1:T(8,128)S(1)}, u32[]{:S(2)}, u32[]{:S(2)}) collective-permute-start(f32[12,3,16,1]{3,0,2,1:T(8,128)S(1)} %get-tuple-element.294), channel_id=1, source_target_pairs={{1,0},{2,1},{3,2},{4,3},{5,4},{6,5},{7,6},{9,8},{10,9},{11,10},{12... | collective-permute-start | bytes 6920 | tf_op jit(solution)/shard_map/ppermute | solution.py:27
  65.0 12.1 %copy-start = (f32[12,3,18,130]{3,0,2,1:T(8,128)}, f32[12,3,18,130]{3,0,2,1:T(8,128)S(1)}, u32[]{:S(2)}) copy-start(f32[12,3,18,130]{3,0,2,1:T(8,128)S(1)} %select_maximum_fusion.8) | copy-start | bytes 1010884
  80.2 21.3 %collective-permute-start.21 = (f32[12,1,16,128]{3,0,2,1:T(8,128)S(1)}, f32[12,1,16,128]{3,0,2,1:T(8,128)S(1)}, u32[]{:S(2)}, u32[]{:S(2)}) collective-permute-start(f32[12,1,16,128]{3,0,2,1:T(8,128)S(1)} %bitcast.551), channel_id=1, source_target_pairs={{0,8},{8,16},{16,24},{24,32},{32,40},{40,48},{48,56},{56,64},{64,7... | collective-permute-start | bytes 294920 | tf_op jit(solution)/shard_map/ppermute | solution.py:26
  82.2 19.4 %collective-permute-start.20 = (f32[12,1,16,128]{3,0,2,1:T(8,128)S(1)}, f32[12,1,16,128]{3,0,2,1:T(8,128)S(1)}, u32[]{:S(2)}, u32[]{:S(2)}) collective-permute-start(f32[12,1,16,128]{3,0,2,1:T(8,128)S(1)} %bitcast.552), channel_id=1, source_target_pairs={{8,0},{16,8},{24,16},{32,24},{40,32},{48,40},{56,48},{64,56},{72,6... | collective-permute-start | bytes 294920 | tf_op jit(solution)/shard_map/ppermute | solution.py:27
  89.1 18.5 %collective-permute-start.9 = (f32[12,1,16,128]{3,0,2,1:T(8,128)S(1)}, f32[12,1,16,128]{3,0,2,1:T(8,128)S(1)}, u32[]{:S(2)}, u32[]{:S(2)}) collective-permute-start(f32[12,1,16,128]{3,0,2,1:T(8,128)S(1)} %fusion.37), channel_id=1, source_target_pairs={{0,8},{8,16},{16,24},{24,32},{32,40},{40,48},{48,56},{56,64},{64,7... | collective-permute-start | bytes 294920 | tf_op jit(solution)/shard_map/ppermute | solution.py:26
  99.6 8.1 %collective-permute-start.8 = (f32[12,1,16,128]{3,0,2,1:T(8,128)S(1)}, f32[12,1,16,128]{3,0,2,1:T(8,128)S(1)}, u32[]{:S(2)}, u32[]{:S(2)}) collective-permute-start(f32[12,1,16,128]{3,0,2,1:T(8,128)S(1)} %fusion.37), channel_id=1, source_target_pairs={{8,0},{16,8},{24,16},{32,24},{40,32},{48,40},{56,48},{64,56},{72,6... | collective-permute-start | bytes 294920 | tf_op jit(solution)/shard_map/ppermute | solution.py:27
  101.5 31.9 %copy-start.5 = (f32[12,1,16,128]{3,0,2,1:T(8,128)}, f32[12,1,16,128]{3,0,2,1:T(8,128)S(1)}, u32[]{:S(2)}) copy-start(f32[12,1,16,128]{3,0,2,1:T(8,128)S(1)} %collective-permute-done.21) | copy-start | bytes 294916
  101.6 31.9 %copy-start.7 = (f32[12,1,16,128]{3,0,2,1:T(8,128)}, f32[12,1,16,128]{3,0,2,1:T(8,128)S(1)}, u32[]{:S(2)}) copy-start(f32[12,1,16,128]{3,0,2,1:T(8,128)S(1)} %collective-permute-done.20) | copy-start | bytes 294916
  101.8 16.0 %collective-permute-start.22 = (f32[12,3,16,1]{3,0,2,1:T(8,128)S(1)}, f32[12,3,16,1]{3,0,2,1:T(8,128)S(1)}, u32[]{:S(2)}, u32[]{:S(2)}) collective-permute-start(f32[12,3,16,1]{3,0,2,1:T(8,128)S(1)} %get-tuple-element.291), channel_id=1, source_target_pairs={{0,1},{1,2},{2,3},{3,4},{4,5},{5,6},{6,7},{8,9},{9,10},{10,11},{11... | collective-permute-start | bytes 6920 | tf_op jit(solution)/shard_map/ppermute | solution.py:26
  103.7 19.3 %collective-permute-start.23 = (f32[12,3,16,1]{3,0,2,1:T(8,128)S(1)}, f32[12,3,16,1]{3,0,2,1:T(8,128)S(1)}, u32[]{:S(2)}, u32[]{:S(2)}) collective-permute-start(f32[12,3,16,1]{3,0,2,1:T(8,128)S(1)} %get-tuple-element.292), channel_id=1, source_target_pairs={{1,0},{2,1},{3,2},{4,3},{5,4},{6,5},{7,6},{9,8},{10,9},{11,10},{12... | collective-permute-start | bytes 6920 | tf_op jit(solution)/shard_map/ppermute | solution.py:27
  107.9 15.5 %collective-permute-start.10 = (f32[12,3,16,1]{3,0,2,1:T(8,128)S(1)}, f32[12,3,16,1]{3,0,2,1:T(8,128)S(1)}, u32[]{:S(2)}, u32[]{:S(2)}) collective-permute-start(f32[12,3,16,1]{3,0,2,1:T(8,128)S(1)} %get-tuple-element.289), channel_id=1, source_target_pairs={{0,1},{1,2},{2,3},{3,4},{4,5},{5,6},{6,7},{8,9},{9,10},{10,11},{11... | collective-permute-start | bytes 6920 | tf_op jit(solution)/shard_map/ppermute | solution.py:26
  115.8 17.3 %collective-permute-start.11 = (f32[12,3,16,1]{3,0,2,1:T(8,128)S(1)}, f32[12,3,16,1]{3,0,2,1:T(8,128)S(1)}, u32[]{:S(2)}, u32[]{:S(2)}) collective-permute-start(f32[12,3,16,1]{3,0,2,1:T(8,128)S(1)} %get-tuple-element.290), channel_id=1, source_target_pairs={{1,0},{2,1},{3,2},{4,3},{5,4},{6,5},{7,6},{9,8},{10,9},{11,10},{12... | collective-permute-start | bytes 6920 | tf_op jit(solution)/shard_map/ppermute | solution.py:27
  123.4 10.1 %copy-start.1 = (f32[12,3,18,130]{3,0,2,1:T(8,128)}, f32[12,3,18,130]{3,0,2,1:T(8,128)S(1)}, u32[]{:S(2)}) copy-start(f32[12,3,18,130]{3,0,2,1:T(8,128)S(1)} %select_maximum_fusion.4) | copy-start | bytes 1010884
  137.4 25.7 %collective-permute-start.25 = (f32[12,1,16,128]{3,0,2,1:T(8,128)S(1)}, f32[12,1,16,128]{3,0,2,1:T(8,128)S(1)}, u32[]{:S(2)}, u32[]{:S(2)}) collective-permute-start(f32[12,1,16,128]{3,0,2,1:T(8,128)S(1)} %bitcast.545), channel_id=1, source_target_pairs={{0,8},{8,16},{16,24},{24,32},{32,40},{40,48},{48,56},{56,64},{64,7... | collective-permute-start | bytes 294920 | tf_op jit(solution)/shard_map/ppermute | solution.py:26
  141.9 21.3 %collective-permute-start.24 = (f32[12,1,16,128]{3,0,2,1:T(8,128)S(1)}, f32[12,1,16,128]{3,0,2,1:T(8,128)S(1)}, u32[]{:S(2)}, u32[]{:S(2)}) collective-permute-start(f32[12,1,16,128]{3,0,2,1:T(8,128)S(1)} %bitcast.546), channel_id=1, source_target_pairs={{8,0},{16,8},{24,16},{32,24},{40,32},{48,40},{56,48},{64,56},{72,6... | collective-permute-start | bytes 294920 | tf_op jit(solution)/shard_map/ppermute | solution.py:27
  146.0 23.3 %collective-permute-start.13 = (f32[12,1,16,128]{3,0,2,1:T(8,128)S(1)}, f32[12,1,16,128]{3,0,2,1:T(8,128)S(1)}, u32[]{:S(2)}, u32[]{:S(2)}) collective-permute-start(f32[12,1,16,128]{3,0,2,1:T(8,128)S(1)} %fusion.36), channel_id=1, source_target_pairs={{0,8},{8,16},{16,24},{24,32},{32,40},{40,48},{48,56},{56,64},{64,7... | collective-permute-start | bytes 294920 | tf_op jit(solution)/shard_map/ppermute | solution.py:26
  161.2 8.0 %collective-permute-start.12 = (f32[12,1,16,128]{3,0,2,1:T(8,128)S(1)}, f32[12,1,16,128]{3,0,2,1:T(8,128)S(1)}, u32[]{:S(2)}, u32[]{:S(2)}) collective-permute-start(f32[12,1,16,128]{3,0,2,1:T(8,128)S(1)} %fusion.36), channel_id=1, source_target_pairs={{8,0},{16,8},{24,16},{32,24},{40,32},{48,40},{56,48},{64,56},{72,6... | collective-permute-start | bytes 294920 | tf_op jit(solution)/shard_map/ppermute | solution.py:27
  163.4 16.0 %collective-permute-start.26 = (f32[12,3,16,1]{3,0,2,1:T(8,128)S(1)}, f32[12,3,16,1]{3,0,2,1:T(8,128)S(1)}, u32[]{:S(2)}, u32[]{:S(2)}) collective-permute-start(f32[12,3,16,1]{3,0,2,1:T(8,128)S(1)} %get-tuple-element.287), channel_id=1, source_target_pairs={{0,1},{1,2},{2,3},{3,4},{4,5},{5,6},{6,7},{8,9},{9,10},{10,11},{11... | collective-permute-start | bytes 6920 | tf_op jit(solution)/shard_map/ppermute | solution.py:26
  165.3 19.3 %collective-permute-start.27 = (f32[12,3,16,1]{3,0,2,1:T(8,128)S(1)}, f32[12,3,16,1]{3,0,2,1:T(8,128)S(1)}, u32[]{:S(2)}, u32[]{:S(2)}) collective-permute-start(f32[12,3,16,1]{3,0,2,1:T(8,128)S(1)} %get-tuple-element.288), channel_id=1, source_target_pairs={{1,0},{2,1},{3,2},{4,3},{5,4},{6,5},{7,6},{9,8},{10,9},{11,10},{12... | collective-permute-start | bytes 6920 | tf_op jit(solution)/shard_map/ppermute | solution.py:27
  169.5 16.5 %collective-permute-start.14 = (f32[12,3,16,1]{3,0,2,1:T(8,128)S(1)}, f32[12,3,16,1]{3,0,2,1:T(8,128)S(1)}, u32[]{:S(2)}, u32[]{:S(2)}) collective-permute-start(f32[12,3,16,1]{3,0,2,1:T(8,128)S(1)} %get-tuple-element.285), channel_id=1, source_target_pairs={{0,1},{1,2},{2,3},{3,4},{4,5},{5,6},{6,7},{8,9},{9,10},{10,11},{11... | collective-permute-start | bytes 6920 | tf_op jit(solution)/shard_map/ppermute | solution.py:26
  177.4 19.4 %collective-permute-start.15 = (f32[12,3,16,1]{3,0,2,1:T(8,128)S(1)}, f32[12,3,16,1]{3,0,2,1:T(8,128)S(1)}, u32[]{:S(2)}, u32[]{:S(2)}) collective-permute-start(f32[12,3,16,1]{3,0,2,1:T(8,128)S(1)} %get-tuple-element.286), channel_id=1, source_target_pairs={{1,0},{2,1},{3,2},{4,3},{5,4},{6,5},{7,6},{9,8},{10,9},{11,10},{12... | collective-permute-start | bytes 6920 | tf_op jit(solution)/shard_map/ppermute | solution.py:27
  185.0 12.3 %copy-start.2 = (f32[12,3,18,130]{3,0,2,1:T(8,128)}, f32[12,3,18,130]{3,0,2,1:T(8,128)S(1)}, u32[]{:S(2)}) copy-start(f32[12,3,18,130]{3,0,2,1:T(8,128)S(1)} %select_maximum_fusion) | copy-start | bytes 1010884
  299.7 25.4 %collective-permute-start.28 = (f32[25,16,128]{2,0,1:T(8,128)}, f32[25,16,128]{2,0,1:T(8,128)}, u32[]{:S(2)}, u32[]{:S(2)}) collective-permute-start(f32[25,16,128]{2,0,1:T(8,128)} %get-tuple-element.269), channel_id=1, source_target_pairs={{8,0},{16,8},{24,16},{32,24},{40,32},{48,40},{56,48},{64,56},{72,6... | collective-permute-start | bytes 614408 | tf_op jit(solution)/shard_map/ppermute | solution.py:16
  305.1 20.0 %collective-permute-start.29 = (f32[25,16,128]{2,0,1:T(8,128)S(1)}, f32[25,16,128]{2,0,1:T(8,128)}, u32[]{:S(2)}, u32[]{:S(2)}) collective-permute-start(f32[25,16,128]{2,0,1:T(8,128)S(1)} %get-tuple-element.270), channel_id=1, source_target_pairs={{0,8},{8,16},{16,24},{24,32},{32,40},{40,48},{48,56},{56,64},{64,7... | collective-permute-start | bytes 614408 | tf_op jit(solution)/shard_map/ppermute | solution.py:16
  307.4 7.2 %collective-permute-start.31 = (f32[25,1,16]{0,2,1:T(8,128)S(1)}, f32[25,1,16]{0,2,1:T(8,128)S(1)}, u32[]{:S(2)}, u32[]{:S(2)}) collective-permute-start(f32[25,1,16]{0,2,1:T(8,128)S(1)} %bitcast.564), channel_id=1, source_target_pairs={{0,1},{1,2},{2,3},{3,4},{4,5},{5,6},{6,7},{8,9},{9,10},{10,11},{11... | collective-permute-start | bytes 4808 | tf_op jit(solution)/shard_map/ppermute | solution.py:16
  312.7 11.6 %collective-permute-start.30 = (f32[25,1,16]{0,2,1:T(8,128)S(1)}, f32[25,1,16]{0,2,1:T(8,128)S(1)}, u32[]{:S(2)}, u32[]{:S(2)}) collective-permute-start(f32[25,1,16]{0,2,1:T(8,128)S(1)} %bitcast.562), channel_id=1, source_target_pairs={{1,0},{2,1},{3,2},{4,3},{5,4},{6,5},{7,6},{9,8},{10,9},{11,10},{12... | collective-permute-start | bytes 4808 | tf_op jit(solution)/shard_map/ppermute | solution.py:16
  335.3 8.8 %copy-start.48 = (f32[1,3,18,130]{3,0,2,1:T(1,128)}, f32[1,3,18,130]{3,0,2,1:T(1,128)S(1)}, u32[]{:S(2)}) copy-start(f32[1,3,18,130]{3,0,2,1:T(1,128)S(1)} %copy.1254) | copy-start | bytes 84244
  337.3 23.4 %collective-permute-start.32 = (f32[25,16,128]{2,0,1:T(8,128)}, f32[25,16,128]{2,0,1:T(8,128)}, u32[]{:S(2)}, u32[]{:S(2)}) collective-permute-start(f32[25,16,128]{2,0,1:T(8,128)} %get-tuple-element.267), channel_id=1, source_target_pairs={{8,0},{16,8},{24,16},{32,24},{40,32},{48,40},{56,48},{64,56},{72,6... | collective-permute-start | bytes 614408 | tf_op jit(solution)/shard_map/ppermute | solution.py:16
  342.2 18.5 %collective-permute-start.33 = (f32[25,16,128]{2,0,1:T(8,128)S(1)}, f32[25,16,128]{2,0,1:T(8,128)}, u32[]{:S(2)}, u32[]{:S(2)}) collective-permute-start(f32[25,16,128]{2,0,1:T(8,128)S(1)} %get-tuple-element.268), channel_id=1, source_target_pairs={{0,8},{8,16},{16,24},{24,32},{32,40},{40,48},{48,56},{56,64},{64,7... | collective-permute-start | bytes 614408 | tf_op jit(solution)/shard_map/ppermute | solution.py:16
  345.1 5.9 %collective-permute-start.35 = (f32[25,1,16]{0,2,1:T(8,128)S(1)}, f32[25,1,16]{0,2,1:T(8,128)}, u32[]{:S(2)}, u32[]{:S(2)}) collective-permute-start(f32[25,1,16]{0,2,1:T(8,128)S(1)} %bitcast.565), channel_id=1, source_target_pairs={{0,1},{1,2},{2,3},{3,4},{4,5},{5,6},{6,7},{8,9},{9,10},{10,11},{11... | collective-permute-start | bytes 4808 | tf_op jit(solution)/shard_map/ppermute | solution.py:16
  347.2 11.9 %collective-permute-start.34 = (f32[25,1,16]{0,2,1:T(8,128)}, f32[25,1,16]{0,2,1:T(8,128)}, u32[]{:S(2)}, u32[]{:S(2)}) collective-permute-start(f32[25,1,16]{0,2,1:T(8,128)} %bitcast.174), channel_id=1, source_target_pairs={{1,0},{2,1},{3,2},{4,3},{5,4},{6,5},{7,6},{9,8},{10,9},{11,10},{12... | collective-permute-start | bytes 4808 | tf_op jit(solution)/shard_map/ppermute | solution.py:16
  365.7 1.6 copy-start.19
  365.7 1.6 copy-start.21
  368.9 1.5 copy-start.64
  368.9 1.5 copy-start.68
  368.9 1.5 copy-start.72
  368.9 1.5 copy-start.76
  368.9 1.5 copy-start.80
  373.4 21.6 %collective-permute-start.36 = (f32[25,16,128]{2,0,1:T(8,128)}, f32[25,16,128]{2,0,1:T(8,128)S(1)}, u32[]{:S(2)}, u32[]{:S(2)}) collective-permute-start(f32[25,16,128]{2,0,1:T(8,128)} %get-tuple-element.265), channel_id=1, source_target_pairs={{8,0},{16,8},{24,16},{32,24},{40,32},{48,40},{56,48},{64,56},{72,6... | collective-permute-start | bytes 614408 | tf_op jit(solution)/shard_map/ppermute | solution.py:16
  378.4 16.6 %collective-permute-start.37 = (f32[25,16,128]{2,0,1:T(8,128)S(1)}, f32[25,16,128]{2,0,1:T(8,128)}, u32[]{:S(2)}, u32[]{:S(2)}) collective-permute-start(f32[25,16,128]{2,0,1:T(8,128)S(1)} %get-tuple-element.266), channel_id=1, source_target_pairs={{0,8},{8,16},{16,24},{24,32},{32,40},{40,48},{48,56},{56,64},{64,7... | collective-permute-start | bytes 614408 | tf_op jit(solution)/shard_map/ppermute | solution.py:16
  380.7 5.9 %collective-permute-start.39 = (f32[25,1,16]{0,2,1:T(8,128)S(1)}, f32[25,1,16]{0,2,1:T(8,128)S(1)}, u32[]{:S(2)}, u32[]{:S(2)}) collective-permute-start(f32[25,1,16]{0,2,1:T(8,128)S(1)} %bitcast.566), channel_id=1, source_target_pairs={{0,1},{1,2},{2,3},{3,4},{4,5},{5,6},{6,7},{8,9},{9,10},{10,11},{11... | collective-permute-start | bytes 4808 | tf_op jit(solution)/shard_map/ppermute | solution.py:16
  383.2 11.6 %collective-permute-start.38 = (f32[25,1,16]{0,2,1:T(8,128)S(1)}, f32[25,1,16]{0,2,1:T(8,128)S(1)}, u32[]{:S(2)}, u32[]{:S(2)}) collective-permute-start(f32[25,1,16]{0,2,1:T(8,128)S(1)} %bitcast.563), channel_id=1, source_target_pairs={{1,0},{2,1},{3,2},{4,3},{5,4},{6,5},{7,6},{9,8},{10,9},{11,10},{12... | collective-permute-start | bytes 4808 | tf_op jit(solution)/shard_map/ppermute | solution.py:16
  (75 other events, 63.0 us)
where the time goes:
time: 401 us; the launch traced here: 399 us
  starting transfers between devices  171 us (43%)
  blocking collectives  84.7 us (21%)
  waiting for transfers between devices  72.8 us (18%)
  local copies, waits for them, and re-layouts  26.4 us (7%)
  other arithmetic  24 us (6%)
  matrix products  14.3 us (4%)
  between operations  4.94 us (1%)
    psum x1, blocking collectives, body(): total = lax.psum(jnp.sum(mismatch * mismatch), ('gx', 'gy'))  84.7 us
    ppermute x14, starting transfers between devices, with_halo(): before = lax.ppermute(last, axis, up)  81.5 us
    ppermute x14, starting transfers between devices, with_halo(): after = lax.ppermute(first, axis, down)  50 us
    ppermute x14, waiting for transfers between devices, with_halo(): after = lax.ppermute(first, axis, down)  47.3 us
    ppermute x12, starting transfers between devices, passed_along(): return lax.ppermute(block, axis, route)  39.9 us
    ppermute x12, waiting for transfers between devices, passed_along(): return lax.ppermute(block, axis, route)  23.2 us
    unnamed x201, local copies, waits for them, and re-layouts  14.5 us
    dot_general x48, matrix products, advance(): jnp.einsum('st,txzy->sxzy', mixers[level], spread, precision=lax.Precisio...  14.3 us
  transfers between devices with their start and end apart: 40, of which 12 were waited for; matrix products, arithmetic and copies ran while one was open for 3% of the time, Pallas kernels for 0%

commit v1 on v0

v1 whole, which is shorter than its diff:
```python
import jax
import jax.numpy as jnp
from jax import lax
from jax.experimental import pallas as pl
from jax.experimental.pallas import tpu as pltpu
from jax.sharding import PartitionSpec as P

MESH = pl.DeviceIdType.MESH
DT = 0.04
STEPS = 3
SPECIES = 12
LAYERS = 4
LANES = 128
ROWS = 16
TORT, DIRE, SOIL = 12, 13, 14


def offsets():
    found = []
    for dx in range(-STEPS, STEPS + 1):
        for dy in (-1, 0, 1):
            depths = STEPS + 1 - abs(dx) - (1 if dy else 0)
            if depths > 0 and (dx or dy):
                found.append((dx, dy, depths))
    return found


ALONG_X = [(dx, dy, depths) for dx, dy, depths in offsets() if dy == 0]
ACROSS = [(dx, dy) for dx, dy, _ in offsets() if dy]
STRIP = {place: i for i, place in enumerate(ACROSS)}
HALO, HALO_ROWS = {}, 0
for dx, _, depths in ALONG_X:
    HALO[dx] = HALO_ROWS
    HALO_ROWS += depths * ROWS
RIM_ROWS = 24
RIM = {dx: i * RIM_ROWS for i, (dx, _, _) in enumerate(ALONG_X)}
FWD_MAIN = {dx: i for i, dx in enumerate(range(-2, 3))}
FWD_EDGE = {dx: 5 + i for i, dx in enumerate(range(-1, 2))}
ADJ_MAIN = {dx: i for i, dx in enumerate(range(-3, 4))}
ADJ_EDGE = {dx: 7 + i for i, dx in enumerate(range(-2, 3))}


def lane(shape):
    return lax.broadcasted_iota(jnp.int32, shape, len(shape) - 1)


def spin(value, by):
    return pltpu.roll(value, by % LANES, value.ndim - 1)


def y_next(main, edge):
    last = lane(main.shape) == LANES - 1
    a, b = spin(main, -1), spin(edge, -1)
    return jnp.where(last, b, a), jnp.where(last, a, b)


def y_prev(main, edge):
    first = lane(main.shape) == 0
    a, b = spin(main, 1), spin(edge, 1)
    return jnp.where(first, b, a), jnp.where(first, a, b)


def pack_strips(tiles):
    group = lane((8, LANES)) // 8
    packed = tiles[0]
    for i, tile in enumerate(tiles[1:], 1):
        packed = jnp.where(group == i, spin(tile, 8 * i), packed)
        packed = jnp.where(group == 15 - i, spin(tile, -8 * i), packed)
    return packed


def unpack_strip(left, right, i):
    return jnp.where(lane((8, LANES)) < LANES // 2, spin(right, -8 * i), spin(left, 8 * i))


def faces(main, edge, closed):
    out = {}
    for kind, field in (("m", main), ("e", edge)):
        for dx in field:
            value = field[dx]
            if dx + 1 in field:
                n = min(value.shape[0], field[dx + 1].shape[0])
                out["x" + kind, dx] = field[dx + 1][:n] - value[:n]
            parts = [value[:1]]
            if value.shape[0] > 1:
                parts.append(value[1:] - value[:-1])
            if closed:
                parts.append(-value[-1:])
            out["z" + kind, dx] = jnp.concatenate(parts, 0) if len(parts) > 1 else parts[0]
    for dx in edge:
        n = edge[dx].shape[0]
        a, b = y_next(main[dx][:n], edge[dx][:n])
        out["ym", dx] = a - main[dx][:n]
        out["ye", dx] = b - edge[dx][:n]
    return out


def times(coeff, diff):
    return {key: coeff[key][: diff[key].shape[0]] * diff[key] for key in diff}


def plus(one, two):
    return {key: one[key] + two[key] for key in one}


def gathered(flux, reach, closed):
    result = []
    for kind, most in (("m", reach), ("e", reach - 1)):
        field = {}
        for dx in range(-most, most + 1):
            depth = flux["z" + kind, dx]
            n = depth.shape[0] - 1
            total = depth[1:] - depth[:-1]
            a, b = y_prev(flux["ym", dx], flux["ye", dx])
            back = a if kind == "m" else b
            side = (
                flux["x" + kind, dx][:n]
                - flux["x" + kind, dx - 1][:n]
                + flux["y" + kind, dx][:n]
                - back[:n]
            )
            if closed:
                total = jnp.concatenate([total[:n] + side, -depth[n:]], 0)
            else:
                total = total + side
            field[dx] = total
        result.append(field)
    return result


def mixed(table, column, value):
    total = None
    for t in range(SPECIES):
        part = table[column, t] * value[:, t // 8 : t // 8 + 1, t % 8 : t % 8 + 1, :]
        total = part if total is None else total + part
    return total


def select_table(table, column, parts, soil):
    masks = [soil == float(level) for level in range(LAYERS)]
    for t in range(SPECIES):
        for half in range(2):
            value = jnp.zeros((8, LANES), jnp.float32)
            for level in range(LAYERS):
                value = jnp.where(masks[level], parts[level, t, half], value)
            table[column, t, half] = value


def kernel(
    nx, ny, c_hbm, m_hbm, d_hbm, mix_hbm, pair_hbm, soil_hbm, obs_hbm, out_ref,
    stage, soil_v, obs_v, mix_ref, pair_ref, block, strip, halo, halo_y, rim_out, rim_strip, rim, rim_y,
    part_out, part_a, part_b,
    square, fwd_parts, adj_parts, fwd, adj,
    local_sem, send_sem, recv_sem,
):
    x, y = lax.axis_index("gx"), lax.axis_index("gy")
    x_hi, x_mid, x_core = x // 8, (x // 2) % 4, x % 2
    y_hi, y_lo = y // 4, y % 4

    def at(dx, dy):
        return (x + dx + nx) % nx, (y + dy + ny) % ny

    group_a = []
    for i in range(1, 16):
        core, mid, high = i % 2, (i // 2) % 4, i // 8
        group_a.append((x_hi * 8 + (x_mid + mid) % 4 * 2 + (x_core + core) % 2, (y_hi + high) % 2 * 4 + y_lo))
    group_b = []
    for i in range(1, 16):
        low, high = i % 4, i // 4
        group_b.append(((x_hi + high) % 4 * 8 + x_mid * 2 + x_core, y_hi * 4 + (y_lo + low) % 4))

    loads = [
        pltpu.make_async_copy(c_hbm.at[:, 0, 0:8], stage.at[0:SPECIES], local_sem.at[0]),
        pltpu.make_async_copy(m_hbm.at[0, 0:8], stage.at[TORT], local_sem.at[1]),
        pltpu.make_async_copy(d_hbm.at[0, 0:8], stage.at[DIRE], local_sem.at[2]),
        pltpu.make_async_copy(soil_hbm, soil_v, local_sem.at[3]),
        pltpu.make_async_copy(mix_hbm, mix_ref, local_sem.at[4]),
        pltpu.make_async_copy(pair_hbm, pair_ref, local_sem.at[5]),
        pltpu.make_async_copy(obs_hbm, obs_v, local_sem.at[6]),
    ]
    for copy in loads:
        copy.start()
    barrier = pltpu.get_barrier_semaphore()
    partners = [at(dx, dy) for dx, dy, _ in offsets()] + group_a + group_b
    for partner in partners:
        pl.semaphore_signal(barrier, inc=1, device_id=partner, device_id_type=MESH)

    stage[SOIL] = jnp.zeros((8, LANES), jnp.float32)
    stage[SOIL + 1] = jnp.zeros((8, LANES), jnp.float32)
    for copy in loads[:4]:
        copy.wait()
    stage[SOIL, 0:1] = soil_v[...].astype(jnp.float32)
    flat = stage.reshape(ROWS * 8, LANES)
    for z in range(STEPS + 1):
        for half in range(2):
            block[pl.ds(z * ROWS + half * 8, 8)] = flat[pl.ds(half * 64 + z, 8, stride=8)]
    strip[...] = pack_strips([block[i * 8 : i * 8 + 8] for i in range(2 * STEPS)])

    pl.semaphore_wait(barrier, len(partners))

    def send(src, dst, number, partner):
        pltpu.make_async_remote_copy(
            src_ref=src, dst_ref=dst, send_sem=send_sem.at[number], recv_sem=recv_sem.at[number],
            device_id=partner, device_id_type=MESH,
        ).start()

    def received(buffer, number):
        pltpu.make_async_copy(buffer, buffer, recv_sem.at[number]).wait()

    def sent(buffer, number):
        pltpu.make_async_copy(buffer, buffer, send_sem.at[number]).wait()

    for dx, dy, depths in ALONG_X:
        rows = depths * ROWS
        send(block.at[pl.ds(0, rows)], halo.at[pl.ds(HALO[-dx], rows)], 0, at(dx, dy))
    for dx, dy in ACROSS:
        send(strip, halo_y.at[STRIP[-dx, -dy]], 1, at(dx, dy))

    for copy in loads[4:]:
        copy.wait()
    square[...] = jnp.zeros((LANES, LANES), jnp.float32)
    diagonal = lax.broadcasted_iota(jnp.int32, (SPECIES, SPECIES), 0) == lax.broadcasted_iota(
        jnp.int32, (SPECIES, SPECIES), 1
    )
    pair = pair_ref[...].astype(jnp.float32)
    for level in range(LAYERS):
        entry = mix_ref[:, level, :]
        square[level * ROWS : level * ROWS + SPECIES, 0:SPECIES] = jnp.where(diagonal, entry, entry * pair)
    plain = square[...]
    turned = plain.T
    for level in range(LAYERS):
        for t in range(SPECIES):
            for half in range(2):
                row = level * ROWS + half * 8
                fwd_parts[level, t, half] = jnp.broadcast_to(plain[row : row + 8, t : t + 1], (8, LANES))
                col = level * ROWS + t
                adj_parts[level, t, half] = jnp.broadcast_to(
                    turned[half * 8 : half * 8 + 8, col : col + 1], (8, LANES)
                )

    received(halo, 0)
    received(halo_y, 1)

    in_x = {dx: jnp.logical_and(x + dx >= 0, x + dx < nx) for dx in range(-STEPS, STEPS + 1)}
    species_row = lax.broadcasted_iota(jnp.int32, (1, 2, 8, LANES), 1) * 8 + lax.broadcasted_iota(
        jnp.int32, (1, 2, 8, LANES), 2
    )
    right_half = lane((8, LANES)) < LANES // 2
    in_y = jnp.where(right_half, y + 1, y - 1)
    in_y = jnp.logical_and(in_y >= 0, in_y < ny)

    def cells(ref, start, depths):
        return ref[pl.ds(start, depths * ROWS)].reshape(depths, 2, 8, LANES)

    def row_of(value, row):
        depths = value.shape[0]
        return jnp.broadcast_to(value[:, row // 8, row % 8 : row % 8 + 1, :], (depths, 8, LANES))

    def zero_unless(valid, value):
        return jnp.where(jnp.broadcast_to(valid, value.shape), value, 0.0)

    def unpack(value, valid):
        depths = value.shape[0]
        state = jnp.where(jnp.broadcast_to(species_row < SPECIES, value.shape), value, 0.0)
        tort, dire = row_of(value, TORT), row_of(value, DIRE)
        soil = row_of(value[:1], SOIL)[0]
        if valid is not None:
            state = zero_unless(valid, state)
            tort, dire = zero_unless(valid, tort), zero_unless(valid, dire)
            soil = jnp.where(valid, soil, -1.0)
        weight = (0.5 * DT) * jnp.exp(tort)
        turn = weight * dire
        shape = (depths, 1, 8, LANES)
        return state, weight.reshape(shape), turn.reshape(shape), dire.reshape(shape), soil

    main, edge = {}, {}
    weight_m, weight_e, turn_m, turn_e, soil_m, soil_e = {}, {}, {}, {}, {}, {}
    for dx in range(-STEPS, STEPS + 1):
        depths = STEPS + 1 - abs(dx)
        raw = cells(block, 0, depths) if dx == 0 else cells(halo, HALO[dx], depths)
        valid = None if dx == 0 else jnp.broadcast_to(in_x[dx], (8, LANES))
        main[dx], weight_m[dx], turn_m[dx], dire, soil_m[dx] = unpack(raw, valid)
        if dx == 0:
            own_dire = dire
        if abs(dx) < STEPS:
            left, right = halo_y[STRIP[dx, -1]], halo_y[STRIP[dx, 1]]
            raw = jnp.stack([unpack_strip(left, right, i) for i in range(2 * (depths - 1))])
            raw = raw.reshape(depths - 1, 2, 8, LANES)
            valid = jnp.logical_and(in_y, jnp.broadcast_to(in_x[dx], (8, LANES)))
            edge[dx], weight_e[dx], turn_e[dx], _, soil_e[dx] = unpack(raw, valid)

    def face_sums(main_w, edge_w, outside):
        out = {}
        for kind, field in (("m", main_w), ("e", edge_w)):
            for dx in field:
                value = field[dx]
                if dx + 1 in field:
                    n = min(value.shape[0], field[dx + 1].shape[0])
                    out["x" + kind, dx] = field[dx + 1][:n] + value[:n]
                parts = [value[:1] + outside]
                if value.shape[0] > 1:
                    parts.append(value[1:] + value[:-1])
                out["z" + kind, dx] = jnp.concatenate(parts, 0) if len(parts) > 1 else parts[0]
        for dx in edge_w:
            n = edge_w[dx].shape[0]
            a, b = y_next(main_w[dx][:n], edge_w[dx][:n])
            out["ym", dx] = a + main_w[dx][:n]
            out["ye", dx] = b + edge_w[dx][:n]
        return out

    coeff = face_sums(weight_m, weight_e, 0.5 * DT)
    slope = face_sums(turn_m, turn_e, 0.0)

    for dx, column in FWD_MAIN.items():
        select_table(fwd, column, fwd_parts, soil_m[dx])
    for dx, column in FWD_EDGE.items():
        select_table(fwd, column, fwd_parts, soil_e[dx])

    diffs, diffs_dot = [], []
    main_dot, edge_dot = None, None
    for k in range(STEPS):
        reach = STEPS - 1 - k
        diff = faces(main, edge, False)
        diffs.append(diff)
        flux = times(coeff, diff)
        flux_dot = times(slope, diff)
        if main_dot is not None:
            diff_dot = faces(main_dot, edge_dot, False)
            flux_dot = plus(flux_dot, times(coeff, diff_dot))
        else:
            diff_dot = None
        diffs_dot.append(diff_dot)
        spread_m, spread_e = gathered(flux, reach, False)
        dot_m, dot_e = gathered(flux_dot, reach, False)
        new = [{}, {}, {}, {}]
        for kind, table, old, old_dot, spread, dot in (
            (0, FWD_MAIN, main, main_dot, spread_m, dot_m),
            (1, FWD_EDGE, edge, edge_dot, spread_e, dot_e),
        ):
            for dx in spread:
                n = spread[dx].shape[0]
                new[kind][dx] = old[dx][:n] + mixed(fwd, table[dx], spread[dx])
                moved = mixed(fwd, table[dx], dot[dx])
                new[2 + kind][dx] = moved if old_dot is None else old_dot[dx][:n] + moved
        main, edge, main_dot, edge_dot = new

    obs = jnp.concatenate([obs_v[s] for s in range(SPECIES)] + [jnp.zeros((ROWS - SPECIES, LANES), jnp.float32)], 0)
    miss = main[0].reshape(ROWS, LANES) - obs
    miss_dot = main_dot[0].reshape(ROWS, LANES)
    square_sum = jnp.sum(miss * miss, 0, keepdims=True)
    cross_sum = jnp.sum(miss * miss_dot, 0, keepdims=True)
    front = lane((1, LANES)) < LANES // 2
    half_row = LANES // 2
    part = jnp.where(front, square_sum + spin(square_sum, half_row), cross_sum + spin(cross_sum, half_row))
    part_out[0] = part
    for slot, partner in enumerate(group_a):
        send(part_out.at[0], part_a.at[slot], 4, partner)

    shared = miss[8:] + pltpu.roll(miss_dot[8:], 4, 0)
    tiles = [miss[:8], miss_dot[:8], shared]
    for i, tile in enumerate(tiles):
        rim_out[i * 8 : i * 8 + 8] = tile
    rim_strip[...] = pack_strips(tiles)
    for dx, dy, _ in ALONG_X:
        send(rim_out, rim.at[pl.ds(RIM[-dx], RIM_ROWS)], 2, at(dx, dy))
    for dx, dy in ACROSS:
        send(rim_strip, rim_y.at[STRIP[-dx, -dy]], 3, at(dx, dy))

    for dx, column in ADJ_MAIN.items():
        select_table(adj, column, adj_parts, soil_m[dx])
    for dx, column in ADJ_EDGE.items():
        select_table(adj, column, adj_parts, soil_e[dx])

    received(part_a, 4)
    part = part + jnp.sum(part_a[...], 0)
    part_out[1] = part
    for slot, partner in enumerate(group_b):
        send(part_out.at[1], part_b.at[slot], 5, partner)

    received(rim, 2)
    received(rim_y, 3)
    lam_m, lam_e, mu_m, mu_e = {}, {}, {}, {}

    def rim_fields(tiles):
        fields = jnp.stack([tiles[0], tiles[2], tiles[1], pltpu.roll(tiles[2], 4, 0)])
        fields = fields.reshape(2, 2, 8, LANES)
        return fields[:1], fields[1:]

    for dx in range(-STEPS, STEPS + 1):
        own = [rim[pl.ds(RIM[dx] + i * 8, 8)] for i in range(3)] if dx else tiles
        lam_m[dx], mu_m[dx] = rim_fields(own)
        if abs(dx) < STEPS:
            left, right = rim_y[STRIP[dx, -1]], rim_y[STRIP[dx, 1]]
            lam_e[dx], mu_e[dx] = rim_fields([unpack_strip(left, right, i) for i in range(3)])

    sums = {}

    def into(key, value):
        value = value[:, 0] + value[:, 1]
        if key in sums:
            old = sums[key]
            n = old.shape[0]
            sums[key] = jnp.concatenate([old + value[:n], value[n:]], 0) if value.shape[0] > n else old + value
        else:
            sums[key] = value

    own = (("xm", 0), ("xm", -1), ("zm", 0), ("ym", 0), ("ye", 0))
    for k in reversed(range(STEPS)):
        reach = STEPS - 1 - k
        u_m = {dx: mixed(adj, ADJ_MAIN[dx], lam_m[dx]) for dx in lam_m}
        v_m = {dx: mixed(adj, ADJ_MAIN[dx], mu_m[dx]) for dx in mu_m}
        u_e = {dx: mixed(adj, ADJ_EDGE[dx], lam_e[dx]) for dx in lam_e}
        v_e = {dx: mixed(adj, ADJ_EDGE[dx], mu_e[dx]) for dx in mu_e}
        diff_u, diff_v = faces(u_m, u_e, True), faces(v_m, v_e, True)
        for key in own:
            du, dv, dc = diff_u[key], diff_v[key], diffs[k][key][: diff_u[key].shape[0]]
            into(("g", key), du * dc)
            second = dv * dc
            if diffs_dot[k] is not None:
                second = second + du * diffs_dot[k][key][: du.shape[0]]
            into(("h", key), second)
        if k == 0:
            break
        need = lambda diff: {
            key: value for key, value in diff.items()
            if key[0][0] == "x" or abs(key[1]) <= (k if key[0] != "ze" else k - 1)
        }
        diff_u, diff_v = need(diff_u), need(diff_v)
        step_m, step_e = gathered(times(coeff, diff_u), k, True)
        dot_m, dot_e = gathered(plus(times(coeff, diff_v), times(slope, diff_u)), k, True)

        def added(old, step):
            n = old.shape[0]
            return jnp.concatenate([old + step[:n], step[n:]], 0)

        lam_m, lam_e = (
            {dx: added(lam_m[dx], step_m[dx]) for dx in step_m},
            {dx: added(lam_e[dx], step_e[dx]) for dx in step_e},
        )
        mu_m, mu_e = (
            {dx: added(mu_m[dx], dot_m[dx]) for dx in dot_m},
            {dx: added(mu_e[dx], dot_e[dx]) for dx in dot_e},
        )

    def per_cell(name):
        y_sum = sums[name, ("ym", 0)]
        side = sums[name, ("xm", 0)] + sums[name, ("xm", -1)] + y_sum
        side = side + y_prev(y_sum, sums[name, ("ye", 0)])[0]
        depth = sums[name, ("zm", 0)]
        n = side.shape[0]
        total = jnp.concatenate([side + depth[:n] + depth[1:], depth[n:]], 0)
        return jnp.sum(total, 1, keepdims=True)

    weight = weight_m[0][:, 0, :1, :]
    plain_part = -weight * per_cell("g")
    dot_part = -weight * per_cell("h") + own_dire[:, 0, :1, :] * plain_part

    received(part_b, 5)
    part = part + jnp.sum(part_b[...], 0)
    total = jnp.sum(jnp.where(front, part, 0.0), 1, keepdims=True)
    cross = jnp.sum(jnp.where(front, 0.0, part), 1, keepdims=True)
    count = float(SPECIES * nx * ny * LANES)
    factor = count / total
    second = -2.0 * count * cross / (total * total)
    zero = jnp.zeros((1, LANES), jnp.float32)
    for z in range(16):
        one, two = (dot_part[z], plain_part[z]) if z <= STEPS else (zero, zero)
        out_ref[0, z : z + 1, :] = factor * one + second * two

    for number, buffer in enumerate((halo, halo_y, rim, rim_y, part_a, part_b)):
        sent(buffer, number)


def solution(mesh):
    nx, ny = mesh.shape["gx"], mesh.shape["gy"]

    def body(c_start, log_tort, direction, mix_inverse, pair_mask, soil_layer, observed):
        f32 = jnp.float32
        hbm = pl.BlockSpec(memory_space=pltpu.HBM)
        vmem = pl.BlockSpec(memory_space=pltpu.VMEM)
        return pl.pallas_call(
            lambda *refs: kernel(nx, ny, *refs),
            out_shape=jax.ShapeDtypeStruct((1, 16, LANES), f32),
            in_specs=[hbm] * 7,
            out_specs=vmem,
            scratch_shapes=[
                pltpu.VMEM((ROWS, 8, LANES), f32),
                pltpu.VMEM((1, LANES), jnp.int32),
                pltpu.VMEM((SPECIES, 1, LANES), f32),
                pltpu.VMEM((SPECIES, LAYERS, SPECIES), f32),
                pltpu.VMEM((SPECIES, SPECIES), jnp.int32),
                pltpu.VMEM(((STEPS + 1) * ROWS, LANES), f32),
                pltpu.VMEM((8, LANES), f32),
                pltpu.VMEM((HALO_ROWS, LANES), f32),
                pltpu.VMEM((len(ACROSS), 8, LANES), f32),
                pltpu.VMEM((RIM_ROWS, LANES), f32),
                pltpu.VMEM((8, LANES), f32),
                pltpu.VMEM((len(ALONG_X) * RIM_ROWS, LANES), f32),
                pltpu.VMEM((len(ACROSS), 8, LANES), f32),
                pltpu.VMEM((2, 1, LANES), f32),
                pltpu.VMEM((15, 1, LANES), f32),
                pltpu.VMEM((15, 1, LANES), f32),
                pltpu.VMEM((LANES, LANES), f32),
                pltpu.VMEM((LAYERS, SPECIES, 2, 8, LANES), f32),
                pltpu.VMEM((LAYERS, SPECIES, 2, 8, LANES), f32),
                pltpu.VMEM((8, SPECIES, 2, 8, LANES), f32),
                pltpu.VMEM((12, SPECIES, 2, 8, LANES), f32),
                pltpu.SemaphoreType.DMA((7,)),
                pltpu.SemaphoreType.DMA((6,)),
                pltpu.SemaphoreType.DMA((6,)),
            ],
            compiler_params=pltpu.CompilerParams(collective_id=0, has_side_effects=True),
        )(c_start, log_tort, direction, mix_inverse.transpose(1, 0, 2), pair_mask, soil_layer, observed)

    return jax.shard_map(
        body,
        mesh=mesh,
        in_specs=(
            P(None, "gx", None, "gy"),
            P("gx", None, "gy"),
            P("gx", None, "gy"),
            P(),
            P(),
            P("gx", "gy"),
            P(None, "gx", "gy"),
        ),
        out_specs=P("gx", None, "gy"),
        check_vma=False,
    )
```

time: 401 us -> 30.5 us (0.08)
  the two profiles are of different devices: /device:TPU:14 before, /device:TPU:1 now
where the time goes in v1:
time: 30.5 us; the launch traced here: 30.4 us
  Pallas kernels  29.1 us (95%)
  local copies, waits for them, and re-layouts  1.3 us (4%)
    pallas_call x1, Pallas kernels, body(): pl.pallas_call(lambda *refs: kernel(nx, ny, *refs), out_shape=jax.ShapeDt...  29.1 us
    unnamed x1, local copies, waits for them, and re-layouts  1.3 us

profile of v1, /device:TPU:1, one launch (start us, length us, event | category | flops | bytes accessed | tf_op | source)
XLA Modules:
  0.0 30.4 jit_solution(17257693423922327639)
XLA Ops:
  0.0 29.1 %shard_map.73 = f32[1,16,128]{2,1,0:T(8,128)} custom-call(f32[12,1,16,128]{3,2,1,0:T(8,128)} %refs_0_.1, f32[1,16,128]{2,1,0:T(8,128)} %refs_1_.1, f32[1,16,128]{2,1,0:T(8,128)} %refs_2_.1, f32[12,4,12]{2,1,0:T(4,128)} %bitcast.1, s32[12,12]{1,0:T(8,128)} %refs_4_.1, s32[1,128]{1,0:T(1,128)} %refs_5_.1, f32[12,1,128]{2,1,0:T(1,128)} %refs_6_.1), custom_call_target="tpu_custom_call" | custom-call | tf_op jit(solution)/shard_map/pallas_call | solution.py:481
  29.1 1.3 %copy.9 = f32[1,16,128]{2,1,0:T(8,128)} copy(f32[1,16,128]{2,1,0:T(8,128)} %shard_map.73) | data formatting | bytes 16384

commit v2 on v1

--- a/solution.py
+++ b/solution.py
@@ -13,6 +13,7 @@
 LANES = 128
 ROWS = 16
 TORT, DIRE, SOIL = 12, 13, 14
+DIRECT = 1
 
 
 def offsets():
@@ -28,6 +29,7 @@
 ALONG_X = [(dx, dy, depths) for dx, dy, depths in offsets() if dy == 0]
 ACROSS = [(dx, dy) for dx, dy, _ in offsets() if dy]
 STRIP = {place: i for i, place in enumerate(ACROSS)}
+SEM = {(dx, dy): i for i, (dx, dy, _) in enumerate(offsets())}
 HALO, HALO_ROWS = {}, 0
 for dx, _, depths in ALONG_X:
     HALO[dx] = HALO_ROWS
@@ -149,25 +151,39 @@
 def kernel(
     nx, ny, c_hbm, m_hbm, d_hbm, mix_hbm, pair_hbm, soil_hbm, obs_hbm, out_ref,
     stage, soil_v, obs_v, mix_ref, pair_ref, block, strip, halo, halo_y, rim_out, rim_strip, rim, rim_y,
-    part_out, part_a, part_b,
+    part_out, part_all, part_b, part_sum,
     square, fwd_parts, adj_parts, fwd, adj,
-    local_sem, send_sem, recv_sem,
+    local_sem, send_sem, recv_sem, ready,
 ):
     x, y = lax.axis_index("gx"), lax.axis_index("gy")
     x_hi, x_mid, x_core = x // 8, (x // 2) % 4, x % 2
     y_hi, y_lo = y // 4, y % 4
 
-    def at(dx, dy):
-        return (x + dx + nx) % nx, (y + dy + ny) % ny
-
-    group_a = []
-    for i in range(1, 16):
-        core, mid, high = i % 2, (i // 2) % 4, i // 8
-        group_a.append((x_hi * 8 + (x_mid + mid) % 4 * 2 + (x_core + core) % 2, (y_hi + high) % 2 * 4 + y_lo))
-    group_b = []
-    for i in range(1, 16):
-        low, high = i % 4, i // 4
-        group_b.append(((x_hi + high) % 4 * 8 + x_mid * 2 + x_core, y_hi * 4 + (y_lo + low) % 4))
+    in_x = {dx: jnp.logical_and(x + dx >= 0, x + dx < nx) for dx in range(-STEPS, STEPS + 1)}
+    all_in_x = jnp.logical_and(x >= STEPS, x < nx - STEPS)
+
+    def neighbours(act, rows=(-1, 1, 0)):
+        for dy in rows:
+            places = [place for place in offsets() if place[1] == dy]
+
+            def row(places=places):
+                @pl.when(all_in_x)
+                def _():
+                    for place in places:
+                        act(*place)
+
+                @pl.when(jnp.logical_not(all_in_x))
+                def _():
+                    for place in places:
+                        pl.when(in_x[place[0]])(lambda place=place: act(*place))
+
+            if dy:
+                pl.when(y > 0 if dy < 0 else y < ny - 1)(row)
+            else:
+                row()
+
+    def signal(semaphore, partner):
+        pl.semaphore_signal(semaphore, inc=1, device_id=partner, device_id_type=MESH)
 
     loads = [
         pltpu.make_async_copy(c_hbm.at[:, 0, 0:8], stage.at[0:SPECIES], local_sem.at[0]),
@@ -178,12 +194,28 @@
         pltpu.make_async_copy(pair_hbm, pair_ref, local_sem.at[5]),
         pltpu.make_async_copy(obs_hbm, obs_v, local_sem.at[6]),
     ]
+    rim[...] = jnp.zeros_like(rim)
+    rim_y[...] = jnp.zeros_like(rim_y)
+    barrier = pltpu.get_barrier_semaphore()
+    neighbours(lambda dx, dy, _: signal(barrier, (x + dx, y + dy)))
     for copy in loads:
         copy.start()
-    barrier = pltpu.get_barrier_semaphore()
-    partners = [at(dx, dy) for dx, dy, _ in offsets()] + group_a + group_b
-    for partner in partners:
-        pl.semaphore_signal(barrier, inc=1, device_id=partner, device_id_type=MESH)
+    group_a = []
+    for i in range(1, 16):
+        core, mid, high = i % 2, (i // 2) % 4, i // 8
+        group_a.append((x_hi * 8 + (x_mid + mid) % 4 * 2 + (x_core + core) % 2, (y_hi + high) % 2 * 4 + y_lo))
+    group_b = []
+    for i in range(1, 16):
+        group_b.append(((x_hi + i // 4) % 4 * 8 + x_mid * 2 + x_core, y_hi * 4 + (y_lo + i % 4) % 4))
+    direct = jnp.logical_and(y_hi == 0, x_mid < DIRECT)
+    for partner in group_a + group_b:
+        signal(barrier, partner)
+    arrivals = len(group_a + group_b)
+    for dx, dy, _ in offsets():
+        there = in_x[dx]
+        if dy:
+            there = jnp.logical_and(there, y > 0 if dy < 0 else y < ny - 1)
+        arrivals = arrivals + there.astype(jnp.int32)
 
     stage[SOIL] = jnp.zeros((8, LANES), jnp.float32)
     stage[SOIL + 1] = jnp.zeros((8, LANES), jnp.float32)
@@ -196,25 +228,38 @@
             block[pl.ds(z * ROWS + half * 8, 8)] = flat[pl.ds(half * 64 + z, 8, stride=8)]
     strip[...] = pack_strips([block[i * 8 : i * 8 + 8] for i in range(2 * STEPS)])
 
-    pl.semaphore_wait(barrier, len(partners))
-
-    def send(src, dst, number, partner):
-        pltpu.make_async_remote_copy(
-            src_ref=src, dst_ref=dst, send_sem=send_sem.at[number], recv_sem=recv_sem.at[number],
+    pl.semaphore_wait(barrier, arrivals)
+
+    @pl.when(direct)
+    def _():
+        for partner in group_a:
+            signal(ready, partner)
+
+
+    def copy_of(src, dst, sems, number, partner):
+        return pltpu.make_async_remote_copy(
+            src_ref=src, dst_ref=dst, send_sem=send_sem.at[sems + number], recv_sem=recv_sem.at[sems + number],
             device_id=partner, device_id_type=MESH,
-        ).start()
-
-    def received(buffer, number):
-        pltpu.make_async_copy(buffer, buffer, recv_sem.at[number]).wait()
-
-    def sent(buffer, number):
-        pltpu.make_async_copy(buffer, buffer, send_sem.at[number]).wait()
-
-    for dx, dy, depths in ALONG_X:
-        rows = depths * ROWS
-        send(block.at[pl.ds(0, rows)], halo.at[pl.ds(HALO[-dx], rows)], 0, at(dx, dy))
-    for dx, dy in ACROSS:
-        send(strip, halo_y.at[STRIP[-dx, -dy]], 1, at(dx, dy))
+        )
+
+    def halo_copy(dx, dy, depths):
+        if dy:
+            src, dst = strip, halo_y.at[STRIP[-dx, -dy]]
+        else:
+            src, dst = block.at[pl.ds(0, depths * ROWS)], halo.at[pl.ds(HALO[-dx], depths * ROWS)]
+        return copy_of(src, dst, 0, SEM[-dx, -dy], (x + dx, y + dy))
+
+    def rim_copy(dx, dy, _):
+        if dy:
+            src, dst = rim_strip, rim_y.at[STRIP[-dx, -dy]]
+        else:
+            src, dst = rim_out, rim.at[pl.ds(RIM[-dx], RIM_ROWS)]
+        return copy_of(src, dst, len(SEM), SEM[-dx, -dy], (x + dx, y + dy))
+
+    def part_copy(index, dst, partner):
+        return copy_of(part_out.at[index % 2], dst, 2 * len(SEM), index, partner)
+
+    neighbours(lambda *place: halo_copy(*place).start())
 
     for copy in loads[4:]:
         copy.wait()
@@ -238,10 +283,11 @@
                     turned[half * 8 : half * 8 + 8, col : col + 1], (8, LANES)
                 )
 
-    received(halo, 0)
-    received(halo_y, 1)
-
-    in_x = {dx: jnp.logical_and(x + dx >= 0, x + dx < nx) for dx in range(-STEPS, STEPS + 1)}
+    def arrived(copy, rows=(-1, 1, 0)):
+        def act(dx, dy, depths):
+            copy(-dx, -dy, depths).wait_recv()
+        neighbours(act, rows)
+
     species_row = lax.broadcasted_iota(jnp.int32, (1, 2, 8, LANES), 1) * 8 + lax.broadcasted_iota(
         jnp.int32, (1, 2, 8, LANES), 2
     )
@@ -275,19 +321,27 @@
 
     main, edge = {}, {}
     weight_m, weight_e, turn_m, turn_e, soil_m, soil_e = {}, {}, {}, {}, {}, {}
-    for dx in range(-STEPS, STEPS + 1):
-        depths = STEPS + 1 - abs(dx)
-        raw = cells(block, 0, depths) if dx == 0 else cells(halo, HALO[dx], depths)
-        valid = None if dx == 0 else jnp.broadcast_to(in_x[dx], (8, LANES))
-        main[dx], weight_m[dx], turn_m[dx], dire, soil_m[dx] = unpack(raw, valid)
-        if dx == 0:
-            own_dire = dire
-        if abs(dx) < STEPS:
-            left, right = halo_y[STRIP[dx, -1]], halo_y[STRIP[dx, 1]]
-            raw = jnp.stack([unpack_strip(left, right, i) for i in range(2 * (depths - 1))])
-            raw = raw.reshape(depths - 1, 2, 8, LANES)
-            valid = jnp.logical_and(in_y, jnp.broadcast_to(in_x[dx], (8, LANES)))
-            edge[dx], weight_e[dx], turn_e[dx], _, soil_e[dx] = unpack(raw, valid)
+    main[0], weight_m[0], turn_m[0], own_dire, soil_m[0] = unpack(cells(block, 0, STEPS + 1), None)
+    select_table(fwd, FWD_MAIN[0], fwd_parts, soil_m[0])
+
+    arrived(halo_copy, (-1, 1))
+    for dx in range(1 - STEPS, STEPS):
+        depths = STEPS - abs(dx)
+        left, right = halo_y[STRIP[dx, -1]], halo_y[STRIP[dx, 1]]
+        raw = jnp.stack([unpack_strip(left, right, i) for i in range(2 * depths)])
+        valid = jnp.logical_and(in_y, jnp.broadcast_to(in_x[dx], (8, LANES)))
+        edge[dx], weight_e[dx], turn_e[dx], _, soil_e[dx] = unpack(raw.reshape(depths, 2, 8, LANES), valid)
+    for dx, column in FWD_EDGE.items():
+        select_table(fwd, column, fwd_parts, soil_e[dx])
+
+    arrived(halo_copy, (0,))
+    for dx, _, depths in ALONG_X:
+        valid = jnp.broadcast_to(in_x[dx], (8, LANES))
+        main[dx], weight_m[dx], turn_m[dx], _, soil_m[dx] = unpack(cells(halo, HALO[dx], depths), valid)
+    main, weight_m, turn_m = ({dx: field[dx] for dx in sorted(field)} for field in (main, weight_m, turn_m))
+    for dx, column in FWD_MAIN.items():
+        if dx:
+            select_table(fwd, column, fwd_parts, soil_m[dx])
 
     def face_sums(main_w, edge_w, outside):
         out = {}
@@ -310,11 +364,6 @@
 
     coeff = face_sums(weight_m, weight_e, 0.5 * DT)
     slope = face_sums(turn_m, turn_e, 0.0)
-
-    for dx, column in FWD_MAIN.items():
-        select_table(fwd, column, fwd_parts, soil_m[dx])
-    for dx, column in FWD_EDGE.items():
-        select_table(fwd, column, fwd_parts, soil_e[dx])
 
     diffs, diffs_dot = [], []
     main_dot, edge_dot = None, None
@@ -354,31 +403,40 @@
     part = jnp.where(front, square_sum + spin(square_sum, half_row), cross_sum + spin(cross_sum, half_row))
     part_out[0] = part
     for slot, partner in enumerate(group_a):
-        send(part_out.at[0], part_a.at[slot], 4, partner)
+        part_copy(0, part_all.at[slot], partner).start()
+    pl.semaphore_wait(ready, 2 * DIRECT - direct.astype(jnp.int32))
+    for mid in range(DIRECT):
+        for core in range(2):
+            step = (core + x_core) % 2 + (mid - x_mid + 4) % 4 * 2 + y_hi * 8
+            for i in range(1, 16):
+                partner = (x_hi + i // 4) % 4 * 8 + mid * 2 + core, (y_lo + i % 4) % 4
+                part_copy(2, part_all.at[i * 16 - 1 + step], partner).start()
 
     shared = miss[8:] + pltpu.roll(miss_dot[8:], 4, 0)
     tiles = [miss[:8], miss_dot[:8], shared]
     for i, tile in enumerate(tiles):
         rim_out[i * 8 : i * 8 + 8] = tile
     rim_strip[...] = pack_strips(tiles)
-    for dx, dy, _ in ALONG_X:
-        send(rim_out, rim.at[pl.ds(RIM[-dx], RIM_ROWS)], 2, at(dx, dy))
-    for dx, dy in ACROSS:
-        send(rim_strip, rim_y.at[STRIP[-dx, -dy]], 3, at(dx, dy))
+    neighbours(lambda *place: rim_copy(*place).start())
 
     for dx, column in ADJ_MAIN.items():
         select_table(adj, column, adj_parts, soil_m[dx])
     for dx, column in ADJ_EDGE.items():
         select_table(adj, column, adj_parts, soil_e[dx])
 
-    received(part_a, 4)
-    part = part + jnp.sum(part_a[...], 0)
-    part_out[1] = part
-    for slot, partner in enumerate(group_b):
-        send(part_out.at[1], part_b.at[slot], 5, partner)
-
-    received(rim, 2)
-    received(rim_y, 3)
+    near, far = part_all.at[pl.ds(0, 15)], part_all.at[pl.ds(15, 240)]
+
+    def all_arrived(buffer, index):
+        pltpu.make_async_copy(buffer, buffer, recv_sem.at[2 * len(SEM) + index]).wait()
+
+    @pl.when(jnp.logical_not(direct))
+    def _():
+        all_arrived(near, 0)
+        part_out[1] = part + jnp.sum(part_all[0:15], 0)
+        for slot, partner in enumerate(group_b):
+            part_copy(1, part_b.at[slot], partner).start()
+
+    arrived(rim_copy)
     lam_m, lam_e, mu_m, mu_e = {}, {}, {}, {}
 
     def rim_fields(tiles):
@@ -455,8 +513,28 @@
     plain_part = -weight * per_cell("g")
     dot_part = -weight * per_cell("h") + own_dire[:, 0, :1, :] * plain_part
 
-    received(part_b, 5)
-    part = part + jnp.sum(part_b[...], 0)
+    neighbours(lambda *place: halo_copy(*place).wait_send())
+    neighbours(lambda *place: rim_copy(*place).wait_send())
+    def all_sent(buffer, index):
+        pltpu.make_async_copy(buffer, buffer, send_sem.at[2 * len(SEM) + index]).wait()
+
+    all_sent(near, 0)
+    all_sent(part_all.at[pl.ds(0, 30 * DIRECT)], 2)
+
+    @pl.when(direct)
+    def _():
+        all_arrived(near, 0)
+        all_arrived(far, 2)
+        rest = part_all[...].reshape(17, 15, 1, LANES)
+        part_sum[...] = part_out[0] + jnp.sum(jnp.sum(rest, 0), 0)
+
+    @pl.when(jnp.logical_not(direct))
+    def _():
+        all_sent(part_b, 1)
+        all_arrived(part_b, 1)
+        part_sum[...] = part_out[1] + jnp.sum(part_b[...], 0)
+
+    part = part_sum[...]
     total = jnp.sum(jnp.where(front, part, 0.0), 1, keepdims=True)
     cross = jnp.sum(jnp.where(front, 0.0, part), 1, keepdims=True)
     count = float(SPECIES * nx * ny * LANES)
@@ -466,9 +544,6 @@
     for z in range(16):
         one, two = (dot_part[z], plain_part[z]) if z <= STEPS else (zero, zero)
         out_ref[0, z : z + 1, :] = factor * one + second * two
-
-    for number, buffer in enumerate((halo, halo_y, rim, rim_y, part_a, part_b)):
-        sent(buffer, number)
 
 
 def solution(mesh):
@@ -498,19 +573,28 @@
                 pltpu.VMEM((len(ALONG_X) * RIM_ROWS, LANES), f32),
                 pltpu.VMEM((len(ACROSS), 8, LANES), f32),
                 pltpu.VMEM((2, 1, LANES), f32),
+                pltpu.VMEM((255, 1, LANES), f32),
                 pltpu.VMEM((15, 1, LANES), f32),
-                pltpu.VMEM((15, 1, LANES), f32),
+                pltpu.VMEM((1, LANES), f32),
                 pltpu.VMEM((LANES, LANES), f32),
                 pltpu.VMEM((LAYERS, SPECIES, 2, 8, LANES), f32),
                 pltpu.VMEM((LAYERS, SPECIES, 2, 8, LANES), f32),
                 pltpu.VMEM((8, SPECIES, 2, 8, LANES), f32),
                 pltpu.VMEM((12, SPECIES, 2, 8, LANES), f32),
                 pltpu.SemaphoreType.DMA((7,)),
-                pltpu.SemaphoreType.DMA((6,)),
-                pltpu.SemaphoreType.DMA((6,)),
+                pltpu.SemaphoreType.DMA((2 * len(SEM) + 3,)),
+                pltpu.SemaphoreType.DMA((2 * len(SEM) + 3,)),
+                pltpu.SemaphoreType.REGULAR,
             ],
-            compiler_params=pltpu.CompilerParams(collective_id=0, has_side_effects=True),
-        )(c_start, log_tort, direction, mix_inverse.transpose(1, 0, 2), pair_mask, soil_layer, observed)
+            compiler_params=pltpu.CompilerParams(
+                collective_id=0, has_side_effects=True, vmem_limit_bytes=32 * 1024 * 1024
+            ),
+        )(*(
+            pltpu.with_memory_space_constraint(value, pltpu.HBM)
+            for value in (
+                c_start, log_tort, direction, mix_inverse.transpose(1, 0, 2), pair_mask, soil_layer, observed,
+            )
+        ))
 
     return jax.shard_map(
         body,

time: 30.5 us -> 25.9 us (0.85)
  Pallas kernels: 29.1 us -> 25.1 us
  local copies, waits for them, and re-layouts: 1.3 us -> 0.6 us
    pallas_call x1, Pallas kernels: 29.1 us -> 25.1 us  [body(): pl.pallas_call(lambda *refs: kernel(nx, ny, *refs), out_shape=jax.ShapeDt...]
    unnamed x1, local copies, waits for them, and re-layouts: 1.3 us -> 0.6 us
where the time goes in v2:
time: 25.9 us; the launch traced here: 25.8 us
  Pallas kernels  25.1 us (97%)
  local copies, waits for them, and re-layouts  0.6 us (2%)
    pallas_call x1, Pallas kernels, body(): pl.pallas_call(lambda *refs: kernel(nx, ny, *refs), out_shape=jax.ShapeDt...  25.1 us
    unnamed x1, local copies, waits for them, and re-layouts  0.6 us

profile of v2, /device:TPU:1, one launch (start us, length us, event | category | flops | bytes accessed | tf_op | source)
XLA Modules:
  0.0 25.8 jit_solution(16676886443246206925)
XLA Ops:
  0.0 25.1 %shard_map.73 = f32[1,16,128]{2,1,0:T(8,128)S(1)} custom-call(f32[12,1,16,128]{3,2,1,0:T(8,128)} %refs_0_.1, f32[1,16,128]{2,1,0:T(8,128)} %refs_1_.1, f32[1,16,128]{2,1,0:T(8,128)} %refs_2_.1, f32[12,4,12]{2,1,0:T(4,128)} %bitcast.1, s32[12,12]{1,0:T(8,128)} %refs_4_.1, s32[1,128]{1,0:T(1,128)} %refs_5_.1, f32[12,1,128]{2,1,0:T(1,128)} %refs_6_.1), custom_call_target="tpu_custom_call" | custom-call | tf_op jit(solution)/shard_map/pallas_call | solution.py:556
  25.2 0.6 %copy.9 = f32[1,16,128]{2,1,0:T(8,128)} copy(f32[1,16,128]{2,1,0:T(8,128)S(1)} %shard_map.73) | data formatting | bytes 16384

commit v3 on v2

--- a/solution.py
+++ b/solution.py
@@ -13,7 +13,6 @@
 LANES = 128
 ROWS = 16
 TORT, DIRE, SOIL = 12, 13, 14
-DIRECT = 1
 
 
 def offsets():
@@ -69,6 +68,20 @@
         packed = jnp.where(group == i, spin(tile, 8 * i), packed)
         packed = jnp.where(group == 15 - i, spin(tile, -8 * i), packed)
     return packed
+
+
+FOLD = 48
+
+
+def fold_strips(packed):
+    place = lane((8, LANES))
+    last = jnp.where(place >= LANES - FOLD, packed, pltpu.roll(spin(packed, -FOLD), 4, 0))
+    first = jnp.where(place < FOLD, packed, pltpu.roll(spin(packed, FOLD), 4, 0))
+    return last[:4], first[:4]
+
+
+def unfold_strips(left, right):
+    return jnp.concatenate([left, spin(left, FOLD)], 0), jnp.concatenate([right, spin(right, -FOLD)], 0)
 
 
 def unpack_strip(left, right, i):
@@ -207,7 +220,7 @@
     group_b = []
     for i in range(1, 16):
         group_b.append(((x_hi + i // 4) % 4 * 8 + x_mid * 2 + x_core, y_hi * 4 + (y_lo + i % 4) % 4))
-    direct = jnp.logical_and(y_hi == 0, x_mid < DIRECT)
+    direct = jnp.logical_and(y_hi == 0, x_mid < 2)
     for partner in group_a + group_b:
         signal(barrier, partner)
     arrivals = len(group_a + group_b)
@@ -226,7 +239,7 @@
     for z in range(STEPS + 1):
         for half in range(2):
             block[pl.ds(z * ROWS + half * 8, 8)] = flat[pl.ds(half * 64 + z, 8, stride=8)]
-    strip[...] = pack_strips([block[i * 8 : i * 8 + 8] for i in range(2 * STEPS)])
+    strip[0], strip[1] = fold_strips(pack_strips([block[i * 8 : i * 8 + 8] for i in range(2 * STEPS)]))
 
     pl.semaphore_wait(barrier, arrivals)
 
@@ -244,14 +257,14 @@
 
     def halo_copy(dx, dy, depths):
         if dy:
-            src, dst = strip, halo_y.at[STRIP[-dx, -dy]]
+            src, dst = strip.at[(1 - dy) // 2], halo_y.at[STRIP[-dx, -dy]]
         else:
             src, dst = block.at[pl.ds(0, depths * ROWS)], halo.at[pl.ds(HALO[-dx], depths * ROWS)]
         return copy_of(src, dst, 0, SEM[-dx, -dy], (x + dx, y + dy))
 
     def rim_copy(dx, dy, _):
         if dy:
-            src, dst = rim_strip, rim_y.at[STRIP[-dx, -dy]]
+            src, dst = rim_strip.at[(1 - dy) // 2], rim_y.at[STRIP[-dx, -dy]]
         else:
             src, dst = rim_out, rim.at[pl.ds(RIM[-dx], RIM_ROWS)]
         return copy_of(src, dst, len(SEM), SEM[-dx, -dy], (x + dx, y + dy))
@@ -259,7 +272,21 @@
     def part_copy(index, dst, partner):
         return copy_of(part_out.at[index % 2], dst, 2 * len(SEM), index, partner)
 
-    neighbours(lambda *place: halo_copy(*place).start())
+    neighbours(lambda *place: halo_copy(*place).start(), (-1, 1))
+
+    def along(places):
+        @pl.when(all_in_x)
+        def _():
+            for place in places:
+                halo_copy(*place).start()
+
+        @pl.when(jnp.logical_not(all_in_x))
+        def _():
+            for place in places:
+                pl.when(in_x[place[0]])(lambda place=place: halo_copy(*place).start())
+
+    pl.when(x % 8 < 4)(lambda: along(ALONG_X))
+    pl.when(x % 8 >= 4)(lambda: along(ALONG_X[::-1]))
 
     for copy in loads[4:]:
         copy.wait()
@@ -327,7 +354,7 @@
     arrived(halo_copy, (-1, 1))
     for dx in range(1 - STEPS, STEPS):
         depths = STEPS - abs(dx)
-        left, right = halo_y[STRIP[dx, -1]], halo_y[STRIP[dx, 1]]
+        left, right = unfold_strips(halo_y[STRIP[dx, -1]], halo_y[STRIP[dx, 1]])
         raw = jnp.stack([unpack_strip(left, right, i) for i in range(2 * depths)])
         valid = jnp.logical_and(in_y, jnp.broadcast_to(in_x[dx], (8, LANES)))
         edge[dx], weight_e[dx], turn_e[dx], _, soil_e[dx] = unpack(raw.reshape(depths, 2, 8, LANES), valid)
@@ -402,21 +429,44 @@
     half_row = LANES // 2
     part = jnp.where(front, square_sum + spin(square_sum, half_row), cross_sum + spin(cross_sum, half_row))
     part_out[0] = part
-    for slot, partner in enumerate(group_a):
-        part_copy(0, part_all.at[slot], partner).start()
-    pl.semaphore_wait(ready, 2 * DIRECT - direct.astype(jnp.int32))
-    for mid in range(DIRECT):
-        for core in range(2):
-            step = (core + x_core) % 2 + (mid - x_mid + 4) % 4 * 2 + y_hi * 8
-            for i in range(1, 16):
-                partner = (x_hi + i // 4) % 4 * 8 + mid * 2 + core, (y_lo + i % 4) % 4
-                part_copy(2, part_all.at[i * 16 - 1 + step], partner).start()
+    pl.semaphore_wait(ready, 4 - direct.astype(jnp.int32))
+
+    def straight(across, mid):
+        north, east = across // 4, across % 4
+        offset = (north - x_hi + 4) % 4 * 4 + (east - y_lo + 4) % 4
+
+        @pl.when(offset > 0)
+        def _():
+            for core in (1, 0):
+                step = (core + x_core) % 2 + (mid - x_mid + 4) % 4 * 2 + y_hi * 8
+                partner = north * 8 + mid * 2 + core, jnp.int32(east)
+                part_copy(2, part_all.at[offset * 16 - 1 + step], partner).start()
+
+    def along_z(height):
+        high, mid = height // 4, height % 4
+        for core in (1, 0):
+            step = (core + x_core) % 2 + (mid - x_mid + 4) % 4 * 2 + (high + y_hi) % 2 * 8
+
+            @pl.when(step > 0)
+            def _(core=core, step=step):
+                partner = x_hi * 8 + mid * 2 + core, high * 4 + y_lo
+                part_copy(0, part_all.at[step - 1], partner).start()
+
+    straight(0, 0)
+    for across in range(4):
+        straight(across, 1)
+    for height in range(8):
+        along_z(height)
+    for across in range(1, 16):
+        straight(across, 0)
+    for across in range(4, 16):
+        straight(across, 1)
 
     shared = miss[8:] + pltpu.roll(miss_dot[8:], 4, 0)
     tiles = [miss[:8], miss_dot[:8], shared]
     for i, tile in enumerate(tiles):
         rim_out[i * 8 : i * 8 + 8] = tile
-    rim_strip[...] = pack_strips(tiles)
+    rim_strip[0], rim_strip[1] = fold_strips(pack_strips(tiles))
     neighbours(lambda *place: rim_copy(*place).start())
 
     for dx, column in ADJ_MAIN.items():
@@ -448,7 +498,7 @@
         own = [rim[pl.ds(RIM[dx] + i * 8, 8)] for i in range(3)] if dx else tiles
         lam_m[dx], mu_m[dx] = rim_fields(own)
         if abs(dx) < STEPS:
-            left, right = rim_y[STRIP[dx, -1]], rim_y[STRIP[dx, 1]]
+            left, right = unfold_strips(rim_y[STRIP[dx, -1]], rim_y[STRIP[dx, 1]])
             lam_e[dx], mu_e[dx] = rim_fields([unpack_strip(left, right, i) for i in range(3)])
 
     sums = {}
@@ -519,7 +569,7 @@
         pltpu.make_async_copy(buffer, buffer, send_sem.at[2 * len(SEM) + index]).wait()
 
     all_sent(near, 0)
-    all_sent(part_all.at[pl.ds(0, 30 * DIRECT)], 2)
+    all_sent(part_all.at[pl.ds(0, 60)], 2)
 
     @pl.when(direct)
     def _():
@@ -565,13 +615,13 @@
                 pltpu.VMEM((SPECIES, LAYERS, SPECIES), f32),
                 pltpu.VMEM((SPECIES, SPECIES), jnp.int32),
                 pltpu.VMEM(((STEPS + 1) * ROWS, LANES), f32),
-                pltpu.VMEM((8, LANES), f32),
+                pltpu.VMEM((2, 4, LANES), f32),
                 pltpu.VMEM((HALO_ROWS, LANES), f32),
-                pltpu.VMEM((len(ACROSS), 8, LANES), f32),
+                pltpu.VMEM((len(ACROSS), 4, LANES), f32),
                 pltpu.VMEM((RIM_ROWS, LANES), f32),
-                pltpu.VMEM((8, LANES), f32),
+                pltpu.VMEM((2, 4, LANES), f32),
                 pltpu.VMEM((len(ALONG_X) * RIM_ROWS, LANES), f32),
-                pltpu.VMEM((len(ACROSS), 8, LANES), f32),
+                pltpu.VMEM((len(ACROSS), 4, LANES), f32),
                 pltpu.VMEM((2, 1, LANES), f32),
                 pltpu.VMEM((255, 1, LANES), f32),
                 pltpu.VMEM((15, 1, LANES), f32),

time: 25.9 us -> 25.1 us (0.969)
  Pallas kernels: 25.1 us -> 24.3 us
    pallas_call x1, Pallas kernels: 25.1 us -> 24.3 us  [body(): pl.pallas_call(lambda *refs: kernel(nx, ny, *refs), out_shape=jax.ShapeDt...]
where the time goes in v3:
time: 25.1 us; the launch traced here: 25 us
  Pallas kernels  24.3 us (97%)
  local copies, waits for them, and re-layouts  0.6 us (2%)
    pallas_call x1, Pallas kernels, body(): pl.pallas_call(lambda *refs: kernel(nx, ny, *refs), out_shape=jax.ShapeDt...  24.3 us
    unnamed x1, local copies, waits for them, and re-layouts  0.6 us

profile of v3, /device:TPU:1, one launch (start us, length us, event | category | flops | bytes accessed | tf_op | source)
XLA Modules:
  0.0 25.0 jit_solution(721538439782330900)
XLA Ops:
  0.0 24.3 %shard_map.73 = f32[1,16,128]{2,1,0:T(8,128)S(1)} custom-call(f32[12,1,16,128]{3,2,1,0:T(8,128)} %refs_0_.1, f32[1,16,128]{2,1,0:T(8,128)} %refs_1_.1, f32[1,16,128]{2,1,0:T(8,128)} %refs_2_.1, f32[12,4,12]{2,1,0:T(4,128)} %bitcast.1, s32[12,12]{1,0:T(8,128)} %refs_4_.1, s32[1,128]{1,0:T(1,128)} %refs_5_.1, f32[12,1,128]{2,1,0:T(1,128)} %refs_6_.1), custom_call_target="tpu_custom_call" | custom-call | tf_op jit(solution)/shard_map/pallas_call | solution.py:606
  24.4 0.6 %copy.9 = f32[1,16,128]{2,1,0:T(8,128)} copy(f32[1,16,128]{2,1,0:T(8,128)S(1)} %shard_map.73) | data formatting | bytes 16384

commit v4 on v3

--- a/solution.py
+++ b/solution.py
@@ -235,7 +235,7 @@
     for copy in loads[:4]:
         copy.wait()
     stage[SOIL, 0:1] = soil_v[...].astype(jnp.float32)
-    flat = stage.reshape(ROWS * 8, LANES)
+    flat = stage.reshape((ROWS + 1) * 8, LANES)
     for z in range(STEPS + 1):
         for half in range(2):
             block[pl.ds(z * ROWS + half * 8, 8)] = flat[pl.ds(half * 64 + z, 8, stride=8)]
@@ -609,7 +609,7 @@
             in_specs=[hbm] * 7,
             out_specs=vmem,
             scratch_shapes=[
-                pltpu.VMEM((ROWS, 8, LANES), f32),
+                pltpu.VMEM((ROWS + 1, 8, LANES), f32),
                 pltpu.VMEM((1, LANES), jnp.int32),
                 pltpu.VMEM((SPECIES, 1, LANES), f32),
                 pltpu.VMEM((SPECIES, LAYERS, SPECIES), f32),

time: 25.1 us -> 25.1 us (level)
  no operation moved by 1% of the time
where the time goes in v4:
time: 25.1 us; the launch traced here: 25 us
  Pallas kernels  24.3 us (97%)
  local copies, waits for them, and re-layouts  0.6 us (2%)
    pallas_call x1, Pallas kernels, body(): pl.pallas_call(lambda *refs: kernel(nx, ny, *refs), out_shape=jax.ShapeDt...  24.3 us
    unnamed x1, local copies, waits for them, and re-layouts  0.6 us

profile of v4, /device:TPU:1, one launch (start us, length us, event | category | flops | bytes accessed | tf_op | source)
XLA Modules:
  0.0 25.0 jit_solution(10328524775105940184)
XLA Ops:
  0.0 24.3 %shard_map.73 = f32[1,16,128]{2,1,0:T(8,128)S(1)} custom-call(f32[12,1,16,128]{3,2,1,0:T(8,128)} %refs_0_.1, f32[1,16,128]{2,1,0:T(8,128)} %refs_1_.1, f32[1,16,128]{2,1,0:T(8,128)} %refs_2_.1, f32[12,4,12]{2,1,0:T(4,128)} %bitcast.1, s32[12,12]{1,0:T(8,128)} %refs_4_.1, s32[1,128]{1,0:T(1,128)} %refs_5_.1, f32[12,1,128]{2,1,0:T(1,128)} %refs_6_.1), custom_call_target="tpu_custom_call" | custom-call | tf_op jit(solution)/shard_map/pallas_call | solution.py:606
  24.4 0.6 %copy.9 = f32[1,16,128]{2,1,0:T(8,128)} copy(f32[1,16,128]{2,1,0:T(8,128)S(1)} %shard_map.73) | data formatting | bytes 16384

commit v5 on v4

--- a/solution.py
+++ b/solution.py
@@ -272,7 +272,7 @@
     def part_copy(index, dst, partner):
         return copy_of(part_out.at[index % 2], dst, 2 * len(SEM), index, partner)
 
-    neighbours(lambda *place: halo_copy(*place).start(), (-1, 1))
+    neighbours(lambda *place: halo_copy(*place).start(), (1, -1))
 
     def along(places):
         @pl.when(all_in_x)

time: 25.1 us -> 25 us (level)
  no operation moved by 1% of the time
where the time goes in v5:
time: 25 us; the launch traced here: 24.9 us
  Pallas kernels  24.3 us (97%)
  local copies, waits for them, and re-layouts  0.6 us (2%)
    pallas_call x1, Pallas kernels, body(): pl.pallas_call(lambda *refs: kernel(nx, ny, *refs), out_shape=jax.ShapeDt...  24.3 us
    unnamed x1, local copies, waits for them, and re-layouts  0.6 us

profile of v5, /device:TPU:1, one launch (start us, length us, event | category | flops | bytes accessed | tf_op | source)
XLA Modules:
  0.0 24.9 jit_solution(1071038293168824423)
XLA Ops:
  0.0 24.3 %shard_map.73 = f32[1,16,128]{2,1,0:T(8,128)S(1)} custom-call(f32[12,1,16,128]{3,2,1,0:T(8,128)} %refs_0_.1, f32[1,16,128]{2,1,0:T(8,128)} %refs_1_.1, f32[1,16,128]{2,1,0:T(8,128)} %refs_2_.1, f32[12,4,12]{2,1,0:T(4,128)} %bitcast.1, s32[12,12]{1,0:T(8,128)} %refs_4_.1, s32[1,128]{1,0:T(1,128)} %refs_5_.1, f32[12,1,128]{2,1,0:T(1,128)} %refs_6_.1), custom_call_target="tpu_custom_call" | custom-call | tf_op jit(solution)/shard_map/pallas_call | solution.py:606
  24.3 0.6 %copy.9 = f32[1,16,128]{2,1,0:T(8,128)} copy(f32[1,16,128]{2,1,0:T(8,128)S(1)} %shard_map.73) | data formatting | bytes 16384

commit v6 on v5

--- a/solution.py
+++ b/solution.py
@@ -574,9 +574,10 @@
     @pl.when(direct)
     def _():
         all_arrived(near, 0)
+        close = part_out[0] + jnp.sum(part_all[0:15], 0)
         all_arrived(far, 2)
-        rest = part_all[...].reshape(17, 15, 1, LANES)
-        part_sum[...] = part_out[0] + jnp.sum(jnp.sum(rest, 0), 0)
+        rest = part_all[15:255].reshape(30, 8, 1, LANES)
+        part_sum[...] = close + jnp.sum(jnp.sum(rest, 0), 0)
 
     @pl.when(jnp.logical_not(direct))
     def _():

time: 25 us -> 25 us (level)
  no operation moved by 1% of the time
where the time goes in v6:
time: 25 us; the launch traced here: 24.9 us
  Pallas kernels  24.3 us (97%)
  local copies, waits for them, and re-layouts  0.6 us (2%)
    pallas_call x1, Pallas kernels, body(): pl.pallas_call(lambda *refs: kernel(nx, ny, *refs), out_shape=jax.ShapeDt...  24.3 us
    unnamed x1, local copies, waits for them, and re-layouts  0.6 us

profile of v6, /device:TPU:1, one launch (start us, length us, event | category | flops | bytes accessed | tf_op | source)
XLA Modules:
  0.0 24.9 jit_solution(4913272731069911779)
XLA Ops:
  0.0 24.3 %shard_map.73 = f32[1,16,128]{2,1,0:T(8,128)S(1)} custom-call(f32[12,1,16,128]{3,2,1,0:T(8,128)} %refs_0_.1, f32[1,16,128]{2,1,0:T(8,128)} %refs_1_.1, f32[1,16,128]{2,1,0:T(8,128)} %refs_2_.1, f32[12,4,12]{2,1,0:T(4,128)} %bitcast.1, s32[12,12]{1,0:T(8,128)} %refs_4_.1, s32[1,128]{1,0:T(1,128)} %refs_5_.1, f32[12,1,128]{2,1,0:T(1,128)} %refs_6_.1), custom_call_target="tpu_custom_call" | custom-call | tf_op jit(solution)/shard_map/pallas_call | solution.py:607
  24.3 0.6 %copy.9 = f32[1,16,128]{2,1,0:T(8,128)} copy(f32[1,16,128]{2,1,0:T(8,128)S(1)} %shard_map.73) | data formatting | bytes 16384
